TPU v7x, 128 devices: a whole 4x4x4 slice. The times are simulated.
128 devices in a mesh: dp: 8 (over x, y_lo), tensor: 16 (over y_hi, z, core).
Axes of the slice: x: 4, y: 4 (y_hi: 2, y_lo: 2; y = y_hi * 2 + y_lo), z: 4, core: 2. Of those that a mesh axis runs over, the one named last changes fastest.
Arguments:
- token_ids: int32 [512, 2], P('dp'), may hold values from 0 to 65535
- embed_table: bfloat16 [65536, 4096], P(('dp', 'tensor')), may hold values from -77 to 77
- in_gain: float32 [4096], replicated, may hold values from 0.25 to 1.75
- in_weight: bfloat16 [4096, 12288], P(None, 'tensor'), may hold values from -0.09375 to 0.09375
- dt_weight: bfloat16 [4096, 32], P(None, 'tensor'), may hold values from -0.09375 to 0.09375
- dt_bias: float32 [32], P('tensor'), may hold values from -2.5 to 0.5
- a_log: float32 [32], P('tensor'), may hold values from -2 to 1.5
- d_skip: float32 [32], P('tensor'), may hold values from 0.5 to 2
- norm_gain: float32 [4096], P('tensor'), may hold values from 0.25 to 1.75
- out_weight: bfloat16 [4096, 4096], P('tensor'), may hold values from -0.125 to 0.125
- next_gain: float32 [4096], replicated, may hold values from 0.25 to 1.75
- ssm_state: float32 [512, 32, 128, 64], P('dp', 'tensor'), may hold values from -4 to 4
- trainer_weight: float32 [4096, 4096], P(('dp', 'tensor')), may hold values from -0.09375 to 0.09375
- head_map: int32 [32, 128], P('tensor'), may hold values from 0 to 127, each once within a row
Outputs:
- new_state: float32 [512, 32, 128, 64], P('dp', 'tensor')
- stream: bfloat16 [512, 2, 4096], P('dp', None, 'tensor')
- normed: bfloat16 [512, 2, 4096], P('dp')
- relaid: float32 [4096, 4096], P('tensor')
Inputs may be any that keep to these rules, and one draw needn't show every extreme that they name: `token_ids`: token ids of the vocabulary of 65536 entries. `head_map`: each row is a permutation of the positions of a head.
All inputs are finite; a program needn't handle non-finite values.
Results may differ from a plain program's by a relative error of at most 0.0066.
Values may be sent and summed in bfloat16 or wider, within the bound.
A program may use at most 128 MiB of HBM per device.

v0:
```python
import jax
import jax.numpy as jnp
from jax import lax
from jax.sharding import PartitionSpec as P

epsilon = 1e-05


def rms_scale(values, gain_row):
    mean_sq = jnp.mean(values * values, axis=-1, keepdims=True)
    return values * lax.rsqrt(mean_sq + epsilon) * gain_row


def per_device(
    token_ids,
    embed_table,
    in_gain,
    in_weight,
    dt_weight,
    dt_bias,
    a_log,
    d_skip,
    norm_gain,
    out_weight,
    next_gain,
    ssm_state,
    trainer_weight,
    head_map,
):
    row_count = token_ids.shape[0]
    step_count = token_ids.shape[1]
    vocab_local = embed_table.shape[0]
    model_width = embed_table.shape[1]
    heads_local = dt_weight.shape[1]
    head_size = ssm_state.shape[2]
    state_size = ssm_state.shape[3]
    tensor_count = lax.axis_size("tensor")
    dp_count = lax.axis_size("dp")
    local_rows = row_count * step_count
    all_ids = lax.all_gather(token_ids, "dp", axis=0, tiled=True).reshape(-1)
    offset = lax.axis_index(("dp", "tensor")) * vocab_local
    columns = lax.broadcasted_iota(jnp.int32, (1, vocab_local), 1)
    onehot = (all_ids[:, None] - offset == columns).astype(jnp.bfloat16)
    lookup_piece = lax.psum_scatter(
        jnp.dot(onehot, embed_table, preferred_element_type=jnp.float32),
        ("dp", "tensor"),
        scatter_dimension=0,
        tiled=True,
    )
    embedded = lax.all_gather(lookup_piece.astype(jnp.bfloat16), "tensor", axis=0, tiled=True)
    embedded_wide = embedded.astype(jnp.float32)
    normed_in = rms_scale(embedded_wide, in_gain).astype(jnp.bfloat16)
    projected = jnp.dot(normed_in, in_weight, preferred_element_type=jnp.float32)
    projected = projected.reshape(
        row_count, step_count, heads_local, 2 * head_size + 2 * state_size
    )
    head_input = projected[..., :head_size]
    head_gate = projected[..., head_size : 2 * head_size]
    write_key = projected[..., 2 * head_size : 2 * head_size + state_size]
    read_query = projected[..., 2 * head_size + state_size :]
    step_size = jax.nn.softplus(
        jnp.dot(normed_in, dt_weight, preferred_element_type=jnp.float32) + dt_bias
    )
    step_size = step_size.reshape(row_count, step_count, heads_local)
    decay_rate = jnp.exp(-step_size * jnp.exp(a_log))
    ssm_now = ssm_state
    outputs = []
    for step_idx in range(step_count):
        scaled_input = step_size[:, step_idx, :, None] * head_input[:, step_idx]
        inject = scaled_input[..., None] * write_key[:, step_idx, :, None, :]
        ssm_now = decay_rate[:, step_idx, :, None, None] * ssm_now + inject
        readout = jnp.einsum(
            "rhin,rhn->rhi", ssm_now, read_query[:, step_idx], precision=lax.Precision.HIGHEST
        )
        outputs.append(readout + d_skip[None, :, None] * head_input[:, step_idx])
    mixer_out = jnp.stack(outputs, axis=1)
    gated_out = mixer_out * jax.nn.silu(head_gate)
    mixed_out = rms_scale(gated_out, norm_gain.reshape(heads_local, head_size)).astype(jnp.bfloat16)
    partial_value = jnp.dot(
        mixed_out.reshape(local_rows, heads_local * head_size),
        out_weight,
        preferred_element_type=jnp.float32,
    )
    share_width = model_width // tensor_count
    share_start = lax.axis_index("tensor") * share_width
    branch = lax.psum(partial_value, "tensor")
    stream_full = (embedded_wide + branch).astype(jnp.bfloat16)
    normed = rms_scale(stream_full.astype(jnp.float32), next_gain).astype(jnp.bfloat16)
    stream = lax.dynamic_slice_in_dim(stream_full, share_start, share_width, 1)
    trainer_rows = trainer_weight.shape[0]
    gathered = lax.all_gather(trainer_weight, "dp", axis=0, tiled=True)
    swapped = lax.all_to_all(gathered, "tensor", split_axis=1, concat_axis=0, tiled=True)
    col_count = swapped.shape[1]
    ordered = (
        swapped.reshape(tensor_count, dp_count, trainer_rows, col_count)
        .transpose(1, 0, 2, 3)
        .reshape(-1, col_count)
    )
    local_weight = ordered.T
    row_index = (lax.broadcasted_iota(jnp.int32, head_map.shape, 0) * head_size + head_map).reshape(
        -1
    )
    relaid = jnp.take(local_weight, row_index, axis=0)
    return (
        ssm_now,
        stream.reshape(row_count, step_count, share_width),
        normed.reshape(row_count, step_count, model_width),
        relaid,
    )


def solution(mesh):
    placed = (
        P("dp", None),
        P(("dp", "tensor"), None),
        P(),
        P(None, "tensor"),
        P(None, "tensor"),
        P("tensor"),
        P("tensor"),
        P("tensor"),
        P("tensor"),
        P("tensor", None),
        P(),
        P("dp", "tensor", None, None),
        P(("dp", "tensor"), None),
        P("tensor", None),
    )
    return jax.shard_map(
        per_device,
        mesh=mesh,
        in_specs=placed,
        out_specs=(
            P("dp", "tensor", None, None),
            P("dp", None, "tensor"),
            P("dp", None, None),
            P("tensor", None),
        ),
        check_vma=False,
    )
```

profile of v0, /device:TPU:1, one launch (start us, length us, event | category | flops | bytes accessed | tf_op | source)
XLA Modules:
  0.0 992.8 jit_solution(14864191597825252515)
XLA Ops:
  8.1 16.3 %all-gather = s32[8,64,2]{1,2,0:T(2,128)S(1)} all-gather(s32[1,64,2]{1,2,0:T(2,128)} %bitcast.82), channel_id=1, replica_groups=mesh['dp'=8,'tensor'=16] {'dp'}, dimensions={0}, use_global_device_ids=true | all-gather | bytes 4608 | tf_op jit(solution)/shard_map/all_gather | solution.py:40
  24.7 10.4 %fusion.11 = f32[1024,4096]{1,0:T(8,128)} fusion(bf16[512,4096]{1,0:T(8,128)(2,1)} %param.15, s32[1024]{0:T(1024)S(1)} %sub.16), kind=kOutput, calls=%fused_computation.21 | convolution fusion | flops 4295491584 | bytes 20975616 | tf_op jit(solution)/shard_map/dot_general | solution.py:45
  35.7 689.2 %reduce-scatter.2.cloned.1.call-done = f32[8,4096]{1,0:T(8,128)} async-done(((f32[1024,4096]{1,0:T(8,128)}), f32[8,4096]{1,0:T(8,128)}) %reduce-scatter.2.cloned.1.call-update) | async-done | bytes 131088 | tf_op jit(solution)/shard_map/reduce_scatter | solution.py:44
  725.0 1.5 convert_element_type.22
  726.6 5.6 copy.86
  732.2 10.0 %all-to-all-start = ((f32[256,16,256]{0,2,1:T(8,128)}), f32[256,16,256]{0,2,1:T(8,128)}, u32[]{:S(2)}, u32[]{:S(2)}) async-start(f32[256,16,256]{0,2,1:T(8,128)} %bitcast.66), calls=%async_computation.1 | async-start | bytes 8388608 | tf_op jit(solution)/shard_map/all_to_all | solution.py:92
  742.3 57.9 %all-gather.4.cloned.1.call-done = bf16[128,4096]{1,0:T(8,128)(2,1)} async-done(((bf16[8,4096]{1,0:T(8,128)(2,1)}), bf16[128,4096]{1,0:T(8,128)(2,1)}) %all-gather.4.cloned.1.call-update) | async-done | bytes 1048592 | tf_op jit(solution)/shard_map/all_gather | solution.py:50
  800.2 1.5 fusion.4
  801.7 1.7 compare_select_fusion.2
  803.8 4.2 fusion.13
  810.6 6.5 multiply_add_fusion
  817.1 2.1 copy-done.2
  819.2 3.7 fusion.29
  822.9 4.2 fusion
  828.0 1.8 fusion.17
  830.0 5.3 copy.87
  835.3 4.7 copy.88
  840.0 5.6 copy.89
  845.6 7.8 gather_fusion
  853.5 5.0 broadcast_select_fusion
  858.4 120.4 %all-reduce.2.cloned.1.call-done = f32[128,4096]{1,0:T(8,128)} async-done(((f32[128,4096]{1,0:T(8,128)}), f32[128,4096]{1,0:T(8,128)}) %all-reduce.2.cloned.1.call-update) | async-done | bytes 2097168 | tf_op jit(solution)/shard_map/psum | solution.py:86
  978.8 2.0 fusion.1
  980.9 1.0 copy-done.4
  982.2 1.5 reshape.131
  (66 shorter events, 6.9 us)
Async XLA Ops:
  8.0 820.0 %copy-start = (bf16[256,4096]{1,0:T(8,128)(2,1)S(1)}, bf16[256,4096]{1,0:T(8,128)(2,1)}, u32[]{:S(2)}) copy-start(bf16[256,4096]{1,0:T(8,128)(2,1)} %param.23) | copy-start | bytes 6291460
  8.0 717.0 %reduce-scatter.2.cloned.1.call-start = ((), (), s32[]{:S(2)}) async-start(), calls=%async_computation.2 | async-start | bytes 16908288 | tf_op jit(solution)/shard_map/reduce_scatter | solution.py:44
  35.1 691.5 %copy-start.12 = (f32[2]{0:T(128)S(1)}, f32[2]{0:T(128)}, u32[]{:S(2)}) copy-start(f32[2]{0:T(128)} %param.20) | copy-start | bytes 28
  35.1 691.5 %all-gather.6.cloned.1.call-start = ((), (), s32[]{:S(2)}) async-start(), calls=%async_computation.5 | async-start | bytes 4718592 | tf_op jit(solution)/shard_map/all_gather | solution.py:91
  35.7 764.5 %all-gather.4.cloned.1.call-start = ((), (), s32[]{:S(2)}) async-start(), calls=%async_computation.3 | async-start | bytes 1114112 | tf_op jit(solution)/shard_map/all_gather | solution.py:50
  732.2 69.5 %copy-start.6 = (f32[4096]{0:T(1024)S(1)}, f32[4096]{0:T(1024)}, u32[]{:S(2)}) copy-start(f32[4096]{0:T(1024)} %param.16) | copy-start | bytes 49156
  732.2 69.5 %copy-start.11 = (bf16[4096,2]{0,1:T(2,128)(2,1)S(1)}, bf16[4096,2]{0,1:T(2,128)(2,1)}, u32[]{:S(2)}) copy-start(bf16[4096,2]{0,1:T(2,128)(2,1)} %param.18) | copy-start | bytes 49156
  732.2 69.5 %copy-start.13 = (f32[2]{0:T(128)S(1)}, f32[2]{0:T(128)}, u32[]{:S(2)}) copy-start(f32[2]{0:T(128)} %param.19) | copy-start | bytes 28
  732.2 97.8 %all-to-all-start = ((f32[256,16,256]{0,2,1:T(8,128)}), f32[256,16,256]{0,2,1:T(8,128)}, u32[]{:S(2)}, u32[]{:S(2)}) async-start(f32[256,16,256]{0,2,1:T(8,128)} %bitcast.66), calls=%async_computation.1 | async-start | bytes 8388608 | tf_op jit(solution)/shard_map/all_to_all | solution.py:92
  742.3 236.6 %all-reduce.2.cloned.1.call-start = ((), (), s32[]{:S(2)}) async-start(), calls=%async_computation.4 | async-start | bytes 4194304 | tf_op jit(solution)/shard_map/psum | solution.py:86
  817.0 2.1 copy-start.2
  817.1 5.9 copy-start.5
  819.2 7.9 copy-start.10
  819.2 8.6 copy-start.8
  827.1 2.8 copy-start.9
  853.5 125.4 %copy-start.3 = (bf16[128,4096]{1,0:T(8,128)(2,1)S(1)}, bf16[128,4096]{1,0:T(8,128)(2,1)}, u32[]{:S(2)}) copy-start(bf16[128,4096]{1,0:T(8,128)(2,1)} %all-gather.4.cloned.1.call-done) | copy-start | bytes 3145732
  853.5 131.7 %copy-start.1 = (bf16[256,4096]{1,0:T(8,128)(2,1)S(1)}, bf16[256,4096]{1,0:T(8,128)(2,1)}, u32[]{:S(2)}) copy-start(bf16[256,4096]{1,0:T(8,128)(2,1)} %param.23) | copy-start | bytes 6291460
  858.4 123.4 %copy-start.7 = (f32[4096]{0:T(1024)S(1)}, f32[4096]{0:T(1024)}, u32[]{:S(2)}) copy-start(f32[4096]{0:T(1024)} %param.24) | copy-start | bytes 49156
  980.8 1.0 copy-start.4
Sparse Core Ops, SparseCore 0:
  35.2 689.6 reduce-scatter.1
Sparse Core Ops, SparseCore 1:
  37.2 92.9 all-gather.5
  726.6 73.5 all-gather.3
  829.9 148.8 all-reduce.1
where the time goes:
time: 994 us; the launch traced here: 993 us
  waiting for transfers between devices  868 us (87%)
  local copies, waits for them, and re-layouts  38.5 us (4%)
  matrix products  25.9 us (3%)
  other arithmetic  17.9 us (2%)
  blocking collectives  16.3 us (2%)
  between operations  15.9 us (2%)
  starting transfers between devices  10.2 us (1%)
    reduce_scatter x1, waiting for transfers between devices, per_device(): lax.psum_scatter(jnp.dot(onehot, embed_table, preferred_element_type=jnp....  689 us
    psum x1, waiting for transfers between devices, per_device(): branch = lax.psum(partial_value, 'tensor')  120 us
    all_gather x1, waiting for transfers between devices, per_device(): lax.all_gather(lookup_piece.astype(jnp.bfloat16), 'tensor', axis=0, tiled...  57.9 us
  transfers between devices with their start and end apart: 5, of which 3 were waited for; matrix products, arithmetic and copies ran while one was open for 6% of the time, Pallas kernels for 0%

commit v1 on v0

v1 whole, which is shorter than its diff:
```python
import functools
import jax
import jax.numpy as jnp
from jax import lax
from jax.experimental import pallas as pl
from jax.experimental.pallas import tpu as pltpu
from jax.sharding import PartitionSpec as P

epsilon = 1e-05
MESH = pl.DeviceIdType.MESH
SLOTS = 8
Z = 4
X = 4


def remote(src, dst, send_sem, recv_sem, **place):
    return pltpu.make_async_remote_copy(
        src_ref=src,
        dst_ref=dst,
        send_sem=send_sem,
        recv_sem=recv_sem,
        device_id=place,
        device_id_type=MESH,
    )


def greet(places):
    barrier = pltpu.get_barrier_semaphore()
    for place in places:
        pl.semaphore_signal(barrier, inc=1, device_id=place, device_id_type=MESH)
    pl.semaphore_wait(barrier, len(places))


def tensor_near(t):
    y, z, c = t // (2 * Z), lax.rem(t // 2, Z), lax.rem(t, 2)
    ahead = [lax.rem(z + o, Z) for o in range(1, Z)]
    behind = [lax.rem(z + Z - o, Z) for o in range(1, Z)]
    place = lambda yy, zz, cc: yy * (2 * Z) + zz * 2 + cc
    return y, z, c, ahead, behind, place


def gather_blocks(buf, t, send, recv):
    y, z, c, ahead, behind, place = tensor_near(t)
    other, across = place(y, z, 1 - c), place(1 - y, z, c)

    def go(block, role, to):
        copy = remote(buf.at[block], buf.at[block], send.at[role], recv.at[role], tensor=to)
        copy.start()
        return copy

    to_across = go(t, 1, across)
    to_z = [go(t, 2 + o, place(y, ahead[o], c)) for o in range(Z - 1)]
    to_core = [go(t, 0, other)]
    to_across.wait_recv()
    passed = [go(across, 5 + o, place(y, ahead[o], c)) for o in range(Z - 1)]
    to_core.append(go(across, 8, other))
    for o in range(Z - 1):
        to_z[o].wait_recv()
        to_core.append(go(place(y, behind[o], c), 9 + o, other))
    for o in range(Z - 1):
        passed[o].wait_recv()
        to_core.append(go(place(1 - y, behind[o], c), 12 + o, other))
    for copy in to_core:
        copy.wait_recv()
    for copy in [to_across] + to_z + passed + to_core:
        copy.wait_send()


def lookup_kernel(first, *refs):
    if first:
        (ids_ref, table_hbm, trainer_hbm, emb, need_ref, swapped, *rest) = refs
        (trainer, swap_out, swap_send, swap_recv, *rest) = rest
    else:
        (ids_ref, start_ref, table_hbm, emb, *rest) = refs
    (table, all_ids, out_d, in_d, out_t, in_t, local, ids_send, ids_recv, d_send, d_recv, t_send, t_recv,
     g_send, g_recv) = rest
    groups, holders = in_d.shape[0], in_t.shape[0]
    rows, vocab, width = ids_ref.shape[1], table.shape[0], table.shape[1]
    block = width // holders
    half = width // 2
    g, t = lax.axis_index("dp"), lax.axis_index("tensor")
    load = pltpu.make_async_copy(table_hbm, table, local.at[0])
    load.start()
    if first:
        load_trainer = pltpu.make_async_copy(trainer_hbm, trainer, local.at[1])
        load_trainer.start()
    all_ids[g] = jnp.broadcast_to(ids_ref[...], (8, rows))
    others_d = [lax.rem(g + o, groups) for o in range(1, groups)]
    others_t = [lax.rem(t + o, holders) for o in range(1, holders)]
    greet([{"dp": d} for d in others_d] + [{"tensor": d} for d in others_t])
    moves = []
    for o, d in enumerate(others_d):
        moves.append(remote(all_ids.at[g], all_ids.at[g], ids_send.at[o], ids_recv.at[o], dp=d))
        moves[-1].start()

    swaps = []
    if first:
        load_trainer.wait()
        for o in range(holders):
            swap_out[o] = trainer[:, o * block : (o + 1) * block].astype(jnp.bfloat16)
        for o, d in enumerate(others_t):
            swaps.append(remote(swap_out.at[d], swapped.at[t], swap_send.at[o], swap_recv.at[o], tensor=d))
            swaps[-1].start()
        swapped[t] = swap_out[t]

    start = 0 if first else start_ref[0:1, 0:1]
    row = ids_ref[...]
    column = jnp.broadcast_to(row, (8, rows)).astype(jnp.float32).T.astype(jnp.int32)[:, 0:1]
    at0 = lax.broadcasted_iota(jnp.int32, (rows, rows), 0)
    at1 = lax.broadcasted_iota(jnp.int32, (rows, rows), 1)

    def order(row, column):
        again = jnp.where((column == row) & (at0 < at1), 1.0, 0.0)
        once = 1.0 - jnp.max(again, axis=0, keepdims=True)
        floor = column - lax.rem(column, vocab)
        before = jnp.where((row >= floor) & (row < column), once, 0.0)
        return jnp.sum(before, axis=1, keepdims=True).astype(jnp.int32)

    slot = order(row, column) - start
    holder = column // vocab
    from_t, from_g = lax.rem(holder, holders), holder // holders
    want = jnp.where((slot >= 0) & (slot < SLOTS), (from_t * groups + from_g) * SLOTS + slot, -1)
    candidates = holders * groups * SLOTS

    for copy in moves:
        copy.wait()

    ids_all = all_ids[0]
    at_g = lax.broadcasted_iota(jnp.int32, (8, rows), 0)
    for gg in range(1, groups):
        ids_all = jnp.where(at_g == gg, all_ids[gg], ids_all)
    columns = ids_all.astype(jnp.float32).T.astype(jnp.int32)
    base = (g * holders + t) * vocab
    at_v = lax.broadcasted_iota(jnp.int32, (rows, vocab), 1)
    pick_g = lax.broadcasted_iota(jnp.int32, (16, vocab), 0)
    held = jnp.zeros((16, vocab), jnp.float32)
    for gg in range(groups):
        asked = jnp.where(columns[:, gg : gg + 1] - base == at_v, 1.0, 0.0)
        held = jnp.where(pick_g == gg, jnp.max(asked, axis=0, keepdims=True), held)
    lower = jnp.where(
        lax.broadcasted_iota(jnp.int32, (vocab, vocab), 0) < lax.broadcasted_iota(jnp.int32, (vocab, vocab), 1),
        1.0,
        0.0,
    ).astype(jnp.bfloat16)
    rank = jnp.dot(held.astype(jnp.bfloat16), lower, preferred_element_type=jnp.float32).astype(jnp.int32) - start
    at_c = lax.broadcasted_iota(jnp.int32, (SLOTS, vocab), 0)
    chosen = jnp.concatenate(
        [
            jnp.where((rank[gg : gg + 1] == at_c) & (held[gg : gg + 1] > 0.5), 1.0, 0.0)
            for gg in range(groups)
        ],
        axis=0,
    ).astype(jnp.bfloat16)
    load.wait()
    step = 512
    for at in range(0, half, step):
        low = jnp.dot(chosen, table[:, at : at + step], preferred_element_type=jnp.float32)
        high = jnp.dot(chosen, table[:, half + at : half + at + step], preferred_element_type=jnp.float32)
        both = jnp.concatenate(
            [low.reshape(groups, SLOTS, step), high.reshape(groups, SLOTS, step)], axis=1
        )
        out_d[:, :, at : at + step] = both.astype(jnp.bfloat16)
    sent = []
    for o, d in enumerate(others_d):
        sent.append(remote(out_d.at[d], in_d.at[g], d_send.at[o], d_recv.at[o], dp=d))
        sent[-1].start()
    in_d[g] = out_d[g]
    if first:
        most = jnp.zeros((1, 1), jnp.int32)
        for gg in range(groups):
            most = jnp.maximum(
                most, jnp.max(order(all_ids[gg][0:1], columns[:, gg : gg + 1]), axis=0, keepdims=True)
            )
        need_ref[...] = jnp.broadcast_to(most + 1, need_ref.shape)
    select = jnp.where(
        want == lax.broadcasted_iota(jnp.int32, (rows, candidates), 1), 1.0, 0.0
    ).astype(jnp.bfloat16)
    for copy in sent:
        copy.wait()
    for o in range(holders):
        part, at = o // (holders // 2), (o % (holders // 2)) * block
        piece = in_d[:, :, at : at + block].astype(jnp.float32)[:, part * SLOTS : (part + 1) * SLOTS]
        out_t[o] = piece.reshape(groups * SLOTS, block).astype(jnp.bfloat16)
    sent = []
    for o, d in enumerate(others_t):
        sent.append(remote(out_t.at[d], in_t.at[t], t_send.at[o], t_recv.at[o], tensor=d))
        sent[-1].start()
    in_t[t] = out_t[t]
    for copy in sent:
        copy.wait()
    found = jnp.dot(select, in_t[...].reshape(candidates, block), preferred_element_type=jnp.float32)
    emb[t] = found.astype(jnp.bfloat16)
    gather_blocks(emb, t, g_send, g_recv)
    for copy in swaps:
        copy.wait()


def lookup(ids, table, groups, holders, trainer=None, start=None):
    first = start is None
    rows = ids.shape[1]
    vocab, width = table.shape
    block = width // holders
    bf16, dma = jnp.bfloat16, pltpu.SemaphoreType.DMA
    vmem, anywhere = pl.BlockSpec(memory_space=pltpu.VMEM), pl.BlockSpec(memory_space=pl.ANY)
    emb_shape = jax.ShapeDtypeStruct((holders, rows, block), bf16)
    scratch = [
        pltpu.VMEM((vocab, width), bf16),
        pltpu.VMEM((groups, 8, rows), jnp.int32),
        pltpu.VMEM((groups, 2 * SLOTS, width // 2), bf16),
        pltpu.VMEM((groups, 2 * SLOTS, width // 2), bf16),
        pltpu.VMEM((holders, groups * SLOTS, block), bf16),
        pltpu.VMEM((holders, groups * SLOTS, block), bf16),
        dma((2,)),
        dma((groups - 1,)),
        dma((groups - 1,)),
        dma((groups - 1,)),
        dma((groups - 1,)),
        dma((holders - 1,)),
        dma((holders - 1,)),
        dma((holders - 1,)),
        dma((holders - 1,)),
    ]
    if first:
        trows = trainer.shape[0]
        args, in_specs = (ids, table, trainer), [vmem, anywhere, anywhere]
        out_shape = (
            emb_shape,
            jax.ShapeDtypeStruct((8, 128), jnp.int32),
            jax.ShapeDtypeStruct((holders, trows, block), bf16),
        )
        scratch = [
            pltpu.VMEM(trainer.shape, jnp.float32),
            pltpu.VMEM((holders, trows, block), bf16),
            dma((holders - 1,)),
            dma((holders - 1,)),
        ] + scratch
    else:
        args, in_specs = (ids, start, table), [vmem, vmem, anywhere]
        out_shape = (emb_shape,)
    return pl.pallas_call(
        functools.partial(lookup_kernel, first),
        out_shape=out_shape,
        in_specs=in_specs,
        out_specs=tuple(vmem for _ in out_shape),
        scratch_shapes=scratch,
        compiler_params=pltpu.CompilerParams(
            collective_id=0 if first else 1, has_side_effects=True, vmem_limit_bytes=40 * 2**20
        ),
        name="lookup_first" if first else "lookup_more",
    )(*args)


def project_kernel(mixed, weight_hbm, emb, swapped_hbm, stream, whole, gathered, weight, out_c, in_c, kept, out_z, in_z,
                   slab, out_y, in_y, local, c_send, c_recv, z_send, z_recv, y_send, y_recv, g_send, g_recv, x_send,
                   x_recv):
    g, t = lax.axis_index("dp"), lax.axis_index("tensor")
    block = whole.shape[2]
    load = pltpu.make_async_copy(weight_hbm, weight, local.at[0])
    load.start()
    own = pltpu.make_async_copy(swapped_hbm, gathered.at[g], local.at[1])
    own.start()
    y, z, c, ahead, behind, place = tensor_near(t)
    x, low = g // 2, lax.rem(g, 2)
    beside = x * 2 + 1 - low
    x_ahead = [lax.rem(x + o, X) * 2 + low for o in range(1, X)]
    other, across = place(y, z, 1 - c), place(1 - y, z, c)
    greet(
        [{"tensor": other}, {"tensor": across}, {"dp": beside}]
        + [{"tensor": place(y, zz, c)} for zz in ahead]
        + [{"dp": d} for d in x_ahead]
    )

    def share(block, role, to):
        copy = remote(gathered.at[block], gathered.at[block], x_send.at[role], x_recv.at[role], dp=to)
        copy.start()
        return copy

    load.wait()
    rows_in = mixed[...]

    def partial_of(k, cc):
        at = place(k % 2, k // 2, cc) * block
        return jnp.dot(rows_in, weight[:, pl.ds(pl.multiple_of(at, block), block)], preferred_element_type=jnp.float32)

    to_core = []
    for k in range(2 * Z):
        out_c[k] = partial_of(k, 1 - c).astype(jnp.bfloat16)
        to_core.append(remote(out_c.at[k], in_c.at[k], c_send.at[k], c_recv.at[k], tensor=other))
        to_core[-1].start()
    own.wait()
    to_beside = share(g, 0, beside)
    to_x = [share(g, 1 + o, x_ahead[o]) for o in range(X - 1)]
    for k in range(2 * Z):
        kept[k // 2, k % 2] = partial_of(k, c)
    for k in range(2 * Z):
        to_core[k].wait_recv()
        total = kept[k // 2, k % 2] + in_c[k].astype(jnp.float32)
        kept[k // 2, k % 2] = total
        out_z[k // 2, k % 2] = total.astype(jnp.bfloat16)
    to_z = []
    for o in range(Z - 1):
        to_z.append(
            remote(out_z.at[ahead[o]], in_z.at[o], z_send.at[o], z_recv.at[o], tensor=place(y, ahead[o], c))
        )
        to_z[-1].start()
    to_beside.wait_recv()
    passed = [share(beside, X + o, x_ahead[o]) for o in range(X - 1)]
    total = kept[z]
    for o in range(Z - 1):
        to_z[o].wait_recv()
        total = total + in_z[o].astype(jnp.float32)
    slab[...] = total
    out_y[...] = slab[1 - y].astype(jnp.bfloat16)
    to_y = remote(out_y, in_y, y_send.at[0], y_recv.at[0], tensor=across)
    to_y.start()
    to_y.wait_recv()
    branch = slab[y] + in_y[...].astype(jnp.float32)
    mine = (emb[t].astype(jnp.float32) + branch).astype(jnp.bfloat16)
    stream[...] = mine
    whole[t] = mine
    gather_blocks(whole, t, g_send, g_recv)
    for copy in to_x + passed:
        copy.wait_recv()
    for copy in to_core + to_z + [to_y, to_beside] + to_x + passed:
        copy.wait_send()


def project(mixed, weight, emb, swapped, groups):
    holders, rows, block = emb.shape
    bf16, f32, dma = jnp.bfloat16, jnp.float32, pltpu.SemaphoreType.DMA
    vmem, anywhere = pl.BlockSpec(memory_space=pltpu.VMEM), pl.BlockSpec(memory_space=pl.ANY)
    return pl.pallas_call(
        project_kernel,
        out_shape=(
            jax.ShapeDtypeStruct((rows, block), bf16),
            jax.ShapeDtypeStruct((holders, rows, block), bf16),
            jax.ShapeDtypeStruct((groups,) + swapped.shape, bf16),
        ),
        in_specs=[vmem, anywhere, vmem, anywhere],
        out_specs=(vmem, vmem, vmem),
        scratch_shapes=[
            pltpu.VMEM(weight.shape, bf16),
            pltpu.VMEM((2 * Z, rows, block), bf16),
            pltpu.VMEM((2 * Z, rows, block), bf16),
            pltpu.VMEM((Z, 2, rows, block), f32),
            pltpu.VMEM((Z, 2, rows, block), bf16),
            pltpu.VMEM((Z - 1, 2, rows, block), bf16),
            pltpu.VMEM((2, rows, block), f32),
            pltpu.VMEM((rows, block), bf16),
            pltpu.VMEM((rows, block), bf16),
            dma((2,)),
            dma((2 * Z,)),
            dma((2 * Z,)),
            dma((Z - 1,)),
            dma((Z - 1,)),
            dma((1,)),
            dma((1,)),
            dma((holders - 1,)),
            dma((holders - 1,)),
            dma((2 * X - 1,)),
            dma((2 * X - 1,)),
        ],
        compiler_params=pltpu.CompilerParams(
            collective_id=2, has_side_effects=True, vmem_limit_bytes=40 * 2**20
        ),
        name="project",
    )(mixed, weight, emb, swapped)


def per_device(
    token_ids,
    embed_table,
    in_gain,
    in_weight,
    dt_weight,
    dt_bias,
    a_log,
    d_skip,
    norm_gain,
    out_weight,
    next_gain,
    ssm_state,
    trainer_weight,
    head_map,
):
    row_count, step_count = token_ids.shape
    model_width = embed_table.shape[1]
    heads_local = dt_weight.shape[1]
    head_size, state_size = ssm_state.shape[2], ssm_state.shape[3]
    holders = lax.axis_size("tensor")
    groups = lax.axis_size("dp")
    rows = row_count * step_count

    ids = token_ids.T.reshape(1, rows)
    emb, need, swapped = lookup(ids, embed_table, groups, holders, trainer=trainer_weight)

    def more(carry):
        done, held = carry
        start = jnp.full((8, 128), done, jnp.int32)
        (found,) = lookup(ids, embed_table, groups, holders, start=start)
        return done + SLOTS, held + found

    _, emb = lax.while_loop(lambda carry: carry[0] < need[0, 0], more, (jnp.int32(SLOTS), emb))

    embedded_wide = emb.transpose(1, 0, 2).reshape(rows, model_width).astype(jnp.float32)
    mean_sq = jnp.mean(embedded_wide * embedded_wide, axis=-1, keepdims=True)
    normed_in = (embedded_wide * lax.rsqrt(mean_sq + epsilon) * in_gain).astype(jnp.bfloat16)
    projected = jnp.dot(normed_in, in_weight, preferred_element_type=jnp.float32)
    projected = projected.reshape(step_count, row_count, heads_local, 2 * head_size + 2 * state_size)
    head_input = projected[..., :head_size]
    head_gate = projected[..., head_size : 2 * head_size]
    write_key = projected[..., 2 * head_size : 2 * head_size + state_size]
    read_query = projected[..., 2 * head_size + state_size :]
    step_size = jax.nn.softplus(jnp.dot(normed_in, dt_weight, preferred_element_type=jnp.float32) + dt_bias)
    step_size = step_size.reshape(step_count, row_count, heads_local)
    decay_rate = jnp.exp(-step_size * jnp.exp(a_log))
    ssm_now = ssm_state
    outputs = []
    for step_idx in range(step_count):
        scaled_input = step_size[step_idx, :, :, None] * head_input[step_idx]
        inject = scaled_input[..., None] * write_key[step_idx, :, :, None, :]
        ssm_now = decay_rate[step_idx, :, :, None, None] * ssm_now + inject
        readout = jnp.sum(ssm_now * read_query[step_idx, :, :, None, :], axis=-1)
        outputs.append(readout + d_skip[None, :, None] * head_input[step_idx])
    gated_out = jnp.stack(outputs, axis=0) * jax.nn.silu(head_gate)
    mean_sq = jnp.mean(gated_out * gated_out, axis=-1, keepdims=True)
    mixed_out = gated_out * lax.rsqrt(mean_sq + epsilon) * norm_gain.reshape(heads_local, head_size)
    mixed_out = mixed_out.astype(jnp.bfloat16).reshape(rows, heads_local * head_size)

    stream, whole, gathered = project(mixed_out, out_weight, emb, swapped, groups)
    wide = whole.astype(jnp.float32)
    mean_sq = jnp.sum(wide * wide, axis=(0, 2), keepdims=True) / model_width
    normed = wide * lax.rsqrt(mean_sq + epsilon) * next_gain.reshape(holders, 1, -1)
    normed = normed.astype(jnp.bfloat16).reshape(holders, step_count, row_count, -1)
    normed = normed.transpose(2, 1, 0, 3).reshape(row_count, step_count, model_width)
    stream = stream.reshape(step_count, row_count, -1).transpose(1, 0, 2)

    units = heads_local * head_size
    row_index = (lax.broadcasted_iota(jnp.int32, head_map.shape, 0) * head_size + head_map).reshape(-1)
    swap = (row_index[:, None] == lax.broadcasted_iota(jnp.int32, (1, units), 1)).astype(jnp.bfloat16)
    relaid = lax.dot_general(
        swap, gathered.reshape(model_width, units), (((1,), (1,)), ((), ())), preferred_element_type=jnp.float32
    )
    return ssm_now, stream, normed, relaid


def solution(mesh):
    placed = (
        P("dp", None),
        P(("dp", "tensor"), None),
        P(),
        P(None, "tensor"),
        P(None, "tensor"),
        P("tensor"),
        P("tensor"),
        P("tensor"),
        P("tensor"),
        P("tensor", None),
        P(),
        P("dp", "tensor", None, None),
        P(("dp", "tensor"), None),
        P("tensor", None),
    )
    return jax.shard_map(
        per_device,
        mesh=mesh,
        in_specs=placed,
        out_specs=(
            P("dp", "tensor", None, None),
            P("dp", None, "tensor"),
            P("dp", None, None),
            P("tensor", None),
        ),
        check_vma=False,
    )
```

time: 994 us -> 115 us (0.12)
  waiting for transfers between devices: 868 us -> 0 us
  Pallas kernels: 0 us -> 72.2 us
  matrix products: 25.9 us -> 8.17 us
  local copies, waits for them, and re-layouts: 38.5 us -> 21.2 us
  blocking collectives: 16.3 us -> 0 us
  between operations: 15.9 us -> 0.93 us
  starting transfers between devices: 10.2 us -> 0 us
    reduce_scatter x1 -> x0, waiting for transfers between devices: 689 us -> none  [per_device(): lax.psum_scatter(jnp.dot(onehot, embed_table, preferred_element_type=jnp....]
    psum x1 -> x0, waiting for transfers between devices: 120 us -> none  [per_device(): branch = lax.psum(partial_value, 'tensor')]
    pallas_call x0 -> x2, Pallas kernels: none -> 72.2 us  [the longest x1 42.2 us: lookup(): pl.pallas_call(functools.partial(lookup_kernel, first), out_shape=out_sha...]
    all_gather x2 -> x0, waiting for transfers between devices: 57.9 us -> none  [the longest x1 57.9 us: per_device(): lax.all_gather(lookup_piece.astype(jnp.bfloat16), 'tensor', axis=0, tiled...]
    dot_general x4 -> x1, matrix products: 20.1 us -> 2.77 us  [per_device(): lax.dot_general(swap, gathered.reshape(model_width, units), (((1,), (1,))...]
    all_gather x1 -> x0, blocking collectives: 16.3 us -> none  [per_device(): all_ids = lax.all_gather(token_ids, 'dp', axis=0, tiled=True).reshape(-1)]
    all_to_all x1 -> x0, starting transfers between devices: 10 us -> none  [per_device(): lax.all_to_all(gathered, 'tensor', split_axis=1, concat_axis=0, tiled=True)]
  transfers between devices with their start and end apart: 5 -> 0, of which waited for: 3 -> 0; matrix products, arithmetic and copies ran while one was open for 6% -> 0% of each run, Pallas kernels for 0% -> 0%
where the time goes in v1:
time: 115 us; the launch traced here: 114 us
  Pallas kernels  72.2 us (63%)
  local copies, waits for them, and re-layouts  21.2 us (18%)
  other arithmetic  10.8 us (9%)
  matrix products  8.17 us (7%)
    pallas_call x1, Pallas kernels, lookup(): pl.pallas_call(functools.partial(lookup_kernel, first), out_shape=out_sha...  42.2 us
    pallas_call x1, Pallas kernels, project(): pl.pallas_call(project_kernel, out_shape=(jax.ShapeDtypeStruct((rows, blo...  30 us
    dot_general x1, local copies, waits for them, and re-layouts, per_device(): jnp.dot(normed_in, in_weight, preferred_element_type=jnp.float32)  8.77 us
    reduce_sum x1, other arithmetic, per_device(): readout = jnp.sum(ssm_now * read_query[step_idx, :, :, None, :], axis=-1)  6.95 us
    dot_general x1, matrix products, per_device(): jnp.dot(normed_in, in_weight, preferred_element_type=jnp.float32)  5.14 us
    dot_general x1, matrix products, per_device(): lax.dot_general(swap, gathered.reshape(model_width, units), (((1,), (1,))...  2.77 us

profile of v1, /device:TPU:1, one launch (start us, length us, event | category | flops | bytes accessed | tf_op | source)
XLA Modules:
  0.0 114.2 jit_solution(1744213130072103675)
XLA Ops:
  0.6 0.8 reshape.114.refs_0_
  1.4 0.7 exp.15
  2.1 0.8 add_bitcast_fusion
  2.8 0.7 mul.272
  3.5 0.7 mul.236
  4.3 1.0 copy-done.2
  5.3 42.2 %lookup_first.1 = (bf16[16,128,256]{2,1,0:T(8,128)(2,1)S(1)}, s32[8,128]{1,0:T(8,128)}, bf16[16,32,256]{2,1,0:T(8,128)(2,1)S(1)}) custom-call(s32[1,128]{1,0:T(1,128)S(1)} %reshape.114.refs_0_, bf16[512,4096]{1,0:T(8,128)(2,1)} %refs_1_.1, f32[32,4096]{1,0:T(8,128)S(1)} %copy-done.2), custom_call_target="tpu_custom_call" | custom-call | tf_op jit(solution)/shard_map/lookup_first/pallas_call | solution.py:240
  47.6 2.0 %while.10 = (s32[]{:T(128)}, bf16[16,128,256]{2,1,0:T(8,128)(2,1)S(1)}, s32[8,128]{1,0:T(8,128)}, s32[1,128]{1,0:T(1,128)S(1)}, bf16[512,4096]{1,0:T(8,128)(2,1)}, /*index=5*/s32[]{:T(128)}) while((s32[]{:T(128)}, bf16[16,128,256]{2,1,0:T(8,128)(2,1)S(1)}, s32[8,128]{1,0:T(8,128)}, s32[1,128]{1,0:T(1,128)S(1)}, bf16[512,4096]{1,0:T(8,128)(2,1)}, ...), condition=%wide.region_1.0_spmd, body=%wide.region_0.0_spmd.sunk | while | flops 524290 | bytes 3149913 | solution.py:403
  47.6 1.2 %slice.83 = s32[1,1]{1,0:T(1,128)} slice(s32[8,128]{1,0:T(8,128)} %get-tuple-element.80), slice={[0:1], [0:1]} | slice | bytes 8 | tf_op jit(solution)/shard_map/while/cond/slice | solution.py:403
  49.6 0.7 copy.46
  50.3 0.6 multiply_reduce_fusion.2
  50.9 0.7 fusion.5
  51.6 0.7 fusion.4
  52.6 0.9 copy.50
  53.5 0.5 reshape.121
  54.5 8.8 %copy.64 = bf16[768,4096]{1,0:T(8,128)(2,1)} copy(bf16[768,4096]{0,1:T(8,128)(2,1)} %bitcast.68) | data formatting | bytes 12582912 | tf_op jit(solution)/shard_map/dot_general | solution.py:408
  63.2 5.1 %fusion.6 = f32[2,64,2,384]{3,1,2,0:T(8,128)S(1)} fusion(bf16[2,384,4096,1]{2,1,0,3:T(8,128)(2,1)} %bitcast.67, bf16[2,64,4096,1]{2,1,0,3:T(8,128)(2,1)S(1)} %reshape.121), kind=kOutput, calls=%fused_computation.16 | convolution fusion | flops 805306368 | bytes 7733248 | tf_op jit(solution)/shard_map/dot_general | solution.py:408
  69.0 6.9 %multiply_reduce_fusion = (f32[64,2,128]{2,1,0:T(2,128)S(1)}, f32[64,2,128,64]{2,3,1,0:T(8,128)}, f32[64,2,128]{2,1,0:T(2,128)S(1)}) fusion(f32[64,2,64]{2,1,0:T(2,128)S(1)} %copy.58, f32[64,2,64]{2,1,0:T(2,128)S(1)} %copy.55, f32[64,2,128]{2,1,0:T(2,128)S(1)} %copy.54, f32[64,2,64]{2,1,0:T(2,128)S(1)} %copy.53, f32[64,2,128]{2,1,0:T(2,128)S(1)} %copy.52, ...), kind=kLoop, calls=%fused_computation | loop fusion | flops 10452992 | bytes 8782848 | tf_op jit(solution)/shard_map/reduce_sum | solution.py:423
  76.4 30.0 %project.1 = (bf16[128,256]{1,0:T(8,128)(2,1)S(1)}, bf16[16,128,256]{2,1,0:T(8,128)(2,1)S(1)}, bf16[8,16,32,256]{3,2,1,0:T(8,128)(2,1)S(1)}) custom-call(bf16[128,256]{1,0:T(8,128)(2,1)S(1)} %bitcast.65, bf16[256,4096]{1,0:T(8,128)(2,1)S(1)} %copy-done.1, bf16[16,128,256]{2,1,0:T(8,128)(2,1)S(1)} %get-tuple-element.40.emb, ...), custom_call_target="tpu_custom_call" | custom-call | tf_op jit(solution)/shard_map/project/pallas_call | solution.py:332
  106.4 0.7 copy.74
  107.4 0.3 fusion.2
  107.8 1.6 %copy.62 = bf16[64,2,16,256]{3,2,1,0:T(8,128)(2,1)} copy(bf16[64,2,16,256]{3,0,1,2:T(8,128)(2,1)S(1)} %bitcast.69) | data formatting | bytes 2097152 | tf_op jit(solution)/shard_map/transpose | solution.py:435
  109.3 2.1 %reshape.118 = bf16[64,2,4096]{2,1,0:T(2,128)(2,1)} reshape(bf16[64,2,16,256]{3,2,1,0:T(8,128)(2,1)} %copy.62) | data formatting | bytes 2097152 | tf_op jit(solution)/shard_map/reshape | solution.py:435
  111.4 2.8 %fusion.8 = f32[256,4096]{1,0:T(8,128)} fusion(bf16[4096,256]{1,0:T(8,128)(2,1)S(1)} %bitcast.64, s32[256]{0:T(256)S(1)} %add_bitcast_fusion), kind=kOutput, calls=%fused_computation.19 | convolution fusion | flops 536936448 | bytes 6292480 | tf_op jit(solution)/shard_map/dot_general | solution.py:441
  (40 shorter events, 1.9 us)
Async XLA Ops:
  0.6 51.7 %copy-start = (bf16[4096,2]{0,1:T(2,128)(2,1)S(1)}, bf16[4096,2]{0,1:T(2,128)(2,1)}, u32[]{:S(2)}) copy-start(bf16[4096,2]{0,1:T(2,128)(2,1)} %param.20) | copy-start | bytes 49156
  4.3 1.0 copy-start.2
  49.6 2.0 %copy-start.4 = (f32[4096]{0:T(1024)S(1)}, f32[4096]{0:T(1024)}, u32[]{:S(2)}) copy-start(f32[4096]{0:T(1024)} %param.18) | copy-start | bytes 49156
  49.6 2.7 %copy-start.7 = (f32[2]{0:T(128)S(1)}, f32[2]{0:T(128)}, u32[]{:S(2)}) copy-start(f32[2]{0:T(128)} %param.21) | copy-start | bytes 28
  63.2 5.7 %copy-start.3 = (f32[64,2,128,64]{2,3,1,0:T(8,128)S(1)}, f32[64,2,128,64]{2,3,1,0:T(8,128)}, u32[]{:S(2)}) copy-start(f32[64,2,128,64]{2,3,1,0:T(8,128)} %param.27) | copy-start | bytes 12582916
  69.0 7.0 %copy-start.6 = (f32[2]{0:T(128)S(1)}, f32[2]{0:T(128)}, u32[]{:S(2)}) copy-start(f32[2]{0:T(128)} %param.23) | copy-start | bytes 28
  69.0 7.2 %copy-start.5 = (f32[256]{0:T(256)S(1)}, f32[256]{0:T(256)}, u32[]{:S(2)}) copy-start(f32[256]{0:T(256)} %param.24) | copy-start | bytes 3076
  69.0 7.4 %copy-start.1 = (bf16[256,4096]{1,0:T(8,128)(2,1)S(1)}, bf16[256,4096]{1,0:T(8,128)(2,1)}, u32[]{:S(2)}) copy-start(bf16[256,4096]{1,0:T(8,128)(2,1)} %weight_hbm.1) | copy-start | bytes 6291460

commit v2 on v1

--- a/solution.py
+++ b/solution.py
@@ -367,6 +367,119 @@
     )(mixed, weight, emb, swapped)
 
 
+def mixer_kernel(heads, emb, gain, weight_hbm, dtw, scalars, ngain, state_hbm, new_hbm, mixed, weight, state, nrm, proj,
+                 kq, xin, xrow, decay, read, w_sem, s_sem, n_sem):
+    holders, rows, block = emb.shape
+    row_count, _, state_size, head_size = state.shape
+    columns = weight.shape[1] // heads
+    steps = rows // row_count
+    parts = w_sem.shape[0]
+    depth = weight.shape[0] // parts
+    chunks = s_sem.shape[0]
+    per = row_count // chunks
+    loads = []
+    for p in range(parts):
+        at = pl.ds(p * depth, depth)
+        loads.append(pltpu.make_async_copy(weight_hbm.at[at], weight.at[at], w_sem.at[p]))
+        loads[-1].start()
+    for p in range(chunks):
+        at = pl.ds(p * per, per)
+        pltpu.make_async_copy(state_hbm.at[at], state.at[at], s_sem.at[p]).start()
+
+    squares = jnp.zeros((rows, block), jnp.float32)
+    for k in range(holders):
+        wide = emb[k].astype(jnp.float32)
+        squares = squares + wide * wide
+    scale = lax.rsqrt(jnp.sum(squares, axis=1, keepdims=True) / (holders * block) + epsilon)
+    for k in range(holders):
+        nrm[:, k * block : (k + 1) * block] = (emb[k].astype(jnp.float32) * scale * gain[k : k + 1]).astype(jnp.bfloat16)
+    narrow = dtw[...].astype(jnp.float32)
+    narrow = jnp.concatenate([narrow, jnp.zeros((16 - heads, narrow.shape[1]), jnp.float32)], axis=0).astype(jnp.bfloat16)
+    steps_raw = lax.dot_general(nrm[...], narrow, (((1,), (1,)), ((), ())), preferred_element_type=jnp.float32)
+    for p in range(parts):
+        loads[p].wait()
+        part = jnp.dot(nrm[:, p * depth : (p + 1) * depth], weight[p * depth : (p + 1) * depth],
+                       preferred_element_type=jnp.float32)
+        proj[...] = part if p == 0 else proj[...] + part
+
+    for h in range(heads):
+        at = h * columns
+        raw = steps_raw[:, h : h + 1] + scalars[0, h]
+        size = jnp.maximum(raw, 0.0) + jnp.log1p(jnp.exp(-jnp.abs(raw)))
+        rate = jnp.exp(-size * jnp.exp(jnp.full((rows, 1), scalars[1, h], jnp.float32)))
+        xin[h] = proj[:, at : at + head_size]
+        xrow[h] = size * proj[:, at : at + head_size]
+        decay[h] = jnp.broadcast_to(rate, (rows, head_size))
+        kq[h] = proj[:, at + 2 * head_size : at + 2 * head_size + 2 * state_size].T
+
+    def chunk(p, carry):
+        at = pl.ds(p * per, per)
+        pltpu.make_async_copy(state_hbm.at[at], state.at[at], s_sem.at[p]).wait()
+        for h in range(heads):
+            turned = pltpu.roll(kq[h], lax.rem(rows - p * per, rows), 1)
+            outs = [[] for _ in range(steps)]
+            for i in range(per):
+                now = state[p * per + i, h]
+                for s in range(steps):
+                    lane = s * row_count + i
+                    r = s * row_count + p * per + i
+                    key = turned[:state_size, lane : lane + 1]
+                    query = turned[state_size:, lane : lane + 1]
+                    now = decay[h, pl.ds(r, 1)] * now + xrow[h, pl.ds(r, 1)] * key
+                    outs[s].append(jnp.sum(now * query, axis=0, keepdims=True))
+                state[p * per + i, h] = now
+            for s in range(steps):
+                read[h, pl.ds(pl.multiple_of(s * row_count + p * per, per), per)] = jnp.concatenate(outs[s], axis=0)
+        pltpu.make_async_copy(state.at[at], new_hbm.at[at], n_sem.at[p]).start()
+        return carry
+
+    lax.fori_loop(0, chunks, chunk, 0)
+    for h in range(heads):
+        at = h * columns
+        out = read[h] + scalars[2, h] * xin[h]
+        gate = proj[:, at + head_size : at + 2 * head_size]
+        out = out * (gate / (1.0 + jnp.exp(-gate)))
+        out = out * lax.rsqrt(jnp.mean(out * out, axis=1, keepdims=True) + epsilon)
+        out = out * ngain[:, h * head_size : (h + 1) * head_size]
+        mixed[:, h * head_size : (h + 1) * head_size] = out.astype(jnp.bfloat16)
+    for p in range(chunks):
+        at = pl.ds(p * per, per)
+        pltpu.make_async_copy(state.at[at], new_hbm.at[at], n_sem.at[p]).wait()
+
+
+def mixer(emb, gain, weight, dtw, scalars, ngain, state):
+    holders, rows, block = emb.shape
+    row_count, heads, state_size, head_size = state.shape
+    bf16, f32, dma = jnp.bfloat16, jnp.float32, pltpu.SemaphoreType.DMA
+    vmem, anywhere = pl.BlockSpec(memory_space=pltpu.VMEM), pl.BlockSpec(memory_space=pl.ANY)
+    smem = pl.BlockSpec(memory_space=pltpu.SMEM)
+    return pl.pallas_call(
+        functools.partial(mixer_kernel, heads),
+        out_shape=(
+            jax.ShapeDtypeStruct(state.shape, f32),
+            jax.ShapeDtypeStruct((rows, heads * head_size), bf16),
+        ),
+        in_specs=[vmem, vmem, anywhere, vmem, smem, vmem, anywhere],
+        out_specs=(anywhere, vmem),
+        scratch_shapes=[
+            pltpu.VMEM(weight.shape, bf16),
+            pltpu.VMEM(state.shape, f32),
+            pltpu.VMEM((rows, holders * block), bf16),
+            pltpu.VMEM((rows, weight.shape[1]), f32),
+            pltpu.VMEM((heads, 2 * state_size, rows), f32),
+            pltpu.VMEM((heads, rows, head_size), f32),
+            pltpu.VMEM((heads, rows, head_size), f32),
+            pltpu.VMEM((heads, rows, head_size), f32),
+            pltpu.VMEM((heads, rows, head_size), f32),
+            dma((4,)),
+            dma((8,)),
+            dma((8,)),
+        ],
+        compiler_params=pltpu.CompilerParams(vmem_limit_bytes=40 * 2**20),
+        name="mixer",
+    )(emb, gain, weight, dtw, scalars, ngain, state)
+
+
 def per_device(
     token_ids,
     embed_table,
@@ -402,30 +515,15 @@
 
     _, emb = lax.while_loop(lambda carry: carry[0] < need[0, 0], more, (jnp.int32(SLOTS), emb))
 
-    embedded_wide = emb.transpose(1, 0, 2).reshape(rows, model_width).astype(jnp.float32)
-    mean_sq = jnp.mean(embedded_wide * embedded_wide, axis=-1, keepdims=True)
-    normed_in = (embedded_wide * lax.rsqrt(mean_sq + epsilon) * in_gain).astype(jnp.bfloat16)
-    projected = jnp.dot(normed_in, in_weight, preferred_element_type=jnp.float32)
-    projected = projected.reshape(step_count, row_count, heads_local, 2 * head_size + 2 * state_size)
-    head_input = projected[..., :head_size]
-    head_gate = projected[..., head_size : 2 * head_size]
-    write_key = projected[..., 2 * head_size : 2 * head_size + state_size]
-    read_query = projected[..., 2 * head_size + state_size :]
-    step_size = jax.nn.softplus(jnp.dot(normed_in, dt_weight, preferred_element_type=jnp.float32) + dt_bias)
-    step_size = step_size.reshape(step_count, row_count, heads_local)
-    decay_rate = jnp.exp(-step_size * jnp.exp(a_log))
-    ssm_now = ssm_state
-    outputs = []
-    for step_idx in range(step_count):
-        scaled_input = step_size[step_idx, :, :, None] * head_input[step_idx]
-        inject = scaled_input[..., None] * write_key[step_idx, :, :, None, :]
-        ssm_now = decay_rate[step_idx, :, :, None, None] * ssm_now + inject
-        readout = jnp.sum(ssm_now * read_query[step_idx, :, :, None, :], axis=-1)
-        outputs.append(readout + d_skip[None, :, None] * head_input[step_idx])
-    gated_out = jnp.stack(outputs, axis=0) * jax.nn.silu(head_gate)
-    mean_sq = jnp.mean(gated_out * gated_out, axis=-1, keepdims=True)
-    mixed_out = gated_out * lax.rsqrt(mean_sq + epsilon) * norm_gain.reshape(heads_local, head_size)
-    mixed_out = mixed_out.astype(jnp.bfloat16).reshape(rows, heads_local * head_size)
+    now, mixed_out = mixer(
+        emb,
+        in_gain.reshape(holders, -1),
+        in_weight,
+        dt_weight.T,
+        jnp.stack([dt_bias, a_log, d_skip]),
+        norm_gain.reshape(1, -1),
+        ssm_state.swapaxes(2, 3),
+    )
 
     stream, whole, gathered = project(mixed_out, out_weight, emb, swapped, groups)
     wide = whole.astype(jnp.float32)
@@ -441,7 +539,7 @@
     relaid = lax.dot_general(
         swap, gathered.reshape(model_width, units), (((1,), (1,)), ((), ())), preferred_element_type=jnp.float32
     )
-    return ssm_now, stream, normed, relaid
+    return now.swapaxes(2, 3), stream, normed, relaid
 
 
 def solution(mesh):

time: 115 us -> 104 us (0.904)
  Pallas kernels: 72.2 us -> 85.3 us
  local copies, waits for them, and re-layouts: 21.2 us -> 11.8 us
  other arithmetic: 10.8 us -> 2.08 us
  matrix products: 8.17 us -> 2.77 us
    pallas_call x0 -> x1, Pallas kernels: none -> 13.1 us  [mixer(): pl.pallas_call(functools.partial(mixer_kernel, heads), out_shape=(jax.Sha...]
    dot_general x1 -> x0, local copies, waits for them, and re-layouts: 8.77 us -> none  [per_device(): jnp.dot(normed_in, in_weight, preferred_element_type=jnp.float32)]
    reduce_sum x3 -> x0, other arithmetic: 7.63 us -> none  [the longest x1 6.95 us: per_device(): readout = jnp.sum(ssm_now * read_query[step_idx, :, :, None, :], axis=-1)]
    dot_general x2 -> x0, matrix products: 5.4 us -> none  [the longest x1 5.14 us: per_device(): jnp.dot(normed_in, in_weight, preferred_element_type=jnp.float32)]
    unnamed x17 -> x12, local copies, waits for them, and re-layouts: 1.1 us -> 6.02 us
    mul x12 -> x0, local copies, waits for them, and re-layouts: 2.24 us -> none  [the longest x2 1.63 us: per_device(): embedded_wide * lax.rsqrt(mean_sq + epsilon) * in_gain]
where the time goes in v2:
time: 104 us
  Pallas kernels  85.3 us (82%)
  local copies, waits for them, and re-layouts  11.8 us (11%)
  matrix products  2.77 us (3%)
  other arithmetic  2.08 us (2%)
    pallas_call x1, Pallas kernels, lookup(): pl.pallas_call(functools.partial(lookup_kernel, first), out_shape=out_sha...  42.2 us
    pallas_call x1, Pallas kernels, project(): pl.pallas_call(project_kernel, out_shape=(jax.ShapeDtypeStruct((rows, blo...  30 us
    pallas_call x1, Pallas kernels, mixer(): pl.pallas_call(functools.partial(mixer_kernel, heads), out_shape=(jax.Sha...  13.1 us
    unnamed x12, local copies, waits for them, and re-layouts  6.02 us
    dot_general x1, matrix products, per_device(): lax.dot_general(swap, gathered.reshape(model_width, units), (((1,), (1,))...  2.77 us

profile of v2, /device:TPU:1, one launch (start us, length us, event | category | flops | bytes accessed | tf_op | source)
XLA Modules:
  0.0 103.5 jit_solution(5426810878917393374)
XLA Ops:
  0.6 0.8 reshape.40.refs_0_
  1.4 0.7 add_bitcast_fusion
  2.1 0.7 pad_maximum_fusion.scalars
  2.8 0.7 reshape.41.gain
  3.6 0.7 mul.31
  4.3 1.0 %copy-done.3 = f32[32,4096]{1,0:T(8,128)S(1)} copy-done((f32[32,4096]{1,0:T(8,128)S(1)}, f32[32,4096]{1,0:T(8,128)}, u32[]{:S(2)}) %copy-start.3) | copy-done | bytes 524312
  5.3 42.2 %lookup_first.1 = (bf16[16,128,256]{2,1,0:T(8,128)(2,1)S(1)}, s32[8,128]{1,0:T(8,128)}, bf16[16,32,256]{2,1,0:T(8,128)(2,1)S(1)}) custom-call(s32[1,128]{1,0:T(1,128)S(1)} %reshape.40.refs_0_, bf16[512,4096]{1,0:T(8,128)(2,1)} %refs_1_.1, f32[32,4096]{1,0:T(8,128)S(1)} %copy-done.3), custom_call_target="tpu_custom_call" | custom-call | tf_op jit(solution)/shard_map/lookup_first/pallas_call | solution.py:240
  47.6 0.0 copy-start.4
  47.6 0.0 copy-start.5
  47.6 2.0 %while.10 = (s32[]{:T(128)}, bf16[16,128,256]{2,1,0:T(8,128)(2,1)S(1)}, s32[8,128]{1,0:T(8,128)}, s32[1,128]{1,0:T(1,128)S(1)}, bf16[512,4096]{1,0:T(8,128)(2,1)}, /*index=5*/s32[]{:T(128)}) while((s32[]{:T(128)}, bf16[16,128,256]{2,1,0:T(8,128)(2,1)S(1)}, s32[8,128]{1,0:T(8,128)}, s32[1,128]{1,0:T(1,128)S(1)}, bf16[512,4096]{1,0:T(8,128)(2,1)}, ...), condition=%wide.region_1.0_spmd, body=%wide.region_0.0_spmd.sunk | while | flops 524290 | bytes 3149913 | solution.py:516
  47.6 1.2 %slice.3 = s32[1,1]{1,0:T(1,128)} slice(s32[8,128]{1,0:T(8,128)} %get-tuple-element.65), slice={[0:1], [0:1]} | slice | bytes 8 | tf_op jit(solution)/shard_map/while/cond/slice | solution.py:516
  49.6 0.0 copy-done.4
  49.7 0.0 copy-start
  49.7 2.8 %copy-done = bf16[4096,768]{1,0:T(8,128)(2,1)S(1)} copy-done((bf16[4096,768]{1,0:T(8,128)(2,1)S(1)}, bf16[4096,768]{1,0:T(8,128)(2,1)}, u32[]{:S(2)}) %copy-start) | copy-done | bytes 6291480
  52.4 2.2 %copy-done.1 = f32[64,2,128,64]{2,3,1,0:T(8,128)S(1)} copy-done((f32[64,2,128,64]{2,3,1,0:T(8,128)S(1)}, f32[64,2,128,64]{2,3,1,0:T(8,128)}, u32[]{:S(2)}) %copy-start.1) | copy-done | bytes 4194328
  54.6 13.1 %mixer.1 = (f32[64,2,64,128]{3,2,1,0:T(8,128)}, bf16[128,256]{1,0:T(8,128)(2,1)S(1)}) custom-call(bf16[16,128,256]{2,1,0:T(8,128)(2,1)S(1)} %get-tuple-element.42.emb, f32[16,256]{1,0:T(8,128)S(1)} %reshape.41.gain, bf16[4096,768]{1,0:T(8,128)(2,1)S(1)} %copy-done, bf16[2,4096]{1,0:T(2,128)(2,1)S(1)} %bitcast.26, f32[3,2]{1,0:T(4,128)S(1)} %pad_maximum_fusion.scalars, ...), custom_call_target="tpu_custom_call" | custom-call | tf_op jit(solution)/shard_map/mixer/pallas_call | solution.py:456
  67.7 0.0 copy-done.2
  67.8 30.0 %project.1 = (bf16[128,256]{1,0:T(8,128)(2,1)S(1)}, bf16[16,128,256]{2,1,0:T(8,128)(2,1)S(1)}, bf16[8,16,32,256]{3,2,1,0:T(8,128)(2,1)S(1)}) custom-call(bf16[128,256]{1,0:T(8,128)(2,1)S(1)} %get-tuple-element.44.mixed, bf16[256,4096]{1,0:T(8,128)(2,1)S(1)} %copy-done.2, bf16[16,128,256]{2,1,0:T(8,128)(2,1)S(1)} %get-tuple-element.42.emb, ...), custom_call_target="tpu_custom_call" | custom-call | tf_op jit(solution)/shard_map/project/pallas_call | solution.py:332
  97.7 0.7 copy.21
  98.4 0.3 fusion
  98.7 0.3 fusion.2
  99.1 0.6 copy.19
  99.7 1.1 %reshape.45 = bf16[64,2,4096]{2,1,0:T(2,128)(2,1)} reshape(bf16[64,2,16,256]{3,2,1,0:T(8,128)(2,1)S(1)} %copy.19) | data formatting | bytes 2097152 | tf_op jit(solution)/shard_map/reshape | solution.py:533
  100.8 2.8 %fusion.3 = f32[256,4096]{1,0:T(8,128)} fusion(bf16[4096,256]{1,0:T(8,128)(2,1)S(1)} %bitcast.24, s32[256]{0:T(256)S(1)} %add_bitcast_fusion), kind=kOutput, calls=%fused_computation.6 | convolution fusion | flops 536936448 | bytes 6292480 | tf_op jit(solution)/shard_map/dot_general | solution.py:539
  (6 shorter events, 0.0 us)
Async XLA Ops:
  4.3 1.0 %copy-start.3 = (f32[32,4096]{1,0:T(8,128)S(1)}, f32[32,4096]{1,0:T(8,128)}, u32[]{:S(2)}) copy-start(f32[32,4096]{1,0:T(8,128)} %refs_2_.1) | copy-start | bytes 1572868
  47.6 2.1 %copy-start.4 = (bf16[4096,2]{0,1:T(2,128)(2,1)S(1)}, bf16[4096,2]{0,1:T(2,128)(2,1)}, u32[]{:S(2)}) copy-start(bf16[4096,2]{0,1:T(2,128)(2,1)} %param.20) | copy-start | bytes 49156
  47.6 2.1 %copy-start.5 = (f32[256]{0:T(256)S(1)}, f32[256]{0:T(256)}, u32[]{:S(2)}) copy-start(f32[256]{0:T(256)} %param.24) | copy-start | bytes 3076
  49.7 2.8 %copy-start = (bf16[4096,768]{1,0:T(8,128)(2,1)S(1)}, bf16[4096,768]{1,0:T(8,128)(2,1)}, u32[]{:S(2)}) copy-start(bf16[4096,768]{1,0:T(8,128)(2,1)} %weight_hbm.2) | copy-start | bytes 18874372
  52.4 2.2 %copy-start.1 = (f32[64,2,128,64]{2,3,1,0:T(8,128)S(1)}, f32[64,2,128,64]{2,3,1,0:T(8,128)}, u32[]{:S(2)}) copy-start(f32[64,2,128,64]{2,3,1,0:T(8,128)} %param.27) | copy-start | bytes 12582916
  54.6 13.1 %copy-start.2 = (bf16[256,4096]{1,0:T(8,128)(2,1)S(1)}, bf16[256,4096]{1,0:T(8,128)(2,1)}, u32[]{:S(2)}) copy-start(bf16[256,4096]{1,0:T(8,128)(2,1)} %weight_hbm.3) | copy-start | bytes 6291460

commit v3 on v2

v3 whole, which is shorter than its diff:
```python
import functools
import jax
import jax.numpy as jnp
from jax import lax
from jax.experimental import pallas as pl
from jax.experimental.pallas import tpu as pltpu
from jax.sharding import PartitionSpec as P

epsilon = 1e-05
MESH = pl.DeviceIdType.MESH
SLOTS = 8
WIDE = 32
Z = 4
X = 4


def remote(src, dst, send_sem, recv_sem, **place):
    return pltpu.make_async_remote_copy(
        src_ref=src,
        dst_ref=dst,
        send_sem=send_sem,
        recv_sem=recv_sem,
        device_id=place,
        device_id_type=MESH,
    )


def greet(places):
    barrier = pltpu.get_barrier_semaphore()
    for place in places:
        pl.semaphore_signal(barrier, inc=1, device_id=place, device_id_type=MESH)
    pl.semaphore_wait(barrier, len(places))


def tensor_near(t):
    y, z, c = t // (2 * Z), lax.rem(t // 2, Z), lax.rem(t, 2)
    ahead = [lax.rem(z + o, Z) for o in range(1, Z)]
    behind = [lax.rem(z + Z - o, Z) for o in range(1, Z)]
    place = lambda yy, zz, cc: yy * (2 * Z) + zz * 2 + cc
    return y, z, c, ahead, behind, place


def gather_blocks(buf, t, send, recv, use=lambda block: None):
    y, z, c, ahead, behind, place = tensor_near(t)
    other, across = place(y, z, 1 - c), place(1 - y, z, c)
    started, to_core = [], []

    def go(block, role, to):
        copy = remote(buf.at[block], buf.at[block], send.at[role], recv.at[role], tensor=to)
        copy.start()
        started.append(copy)
        return copy

    def core(block, role):
        to_core.append((go(block, role, other), role))

    to_across = go(t, 1, across)
    to_z = {o: go(t, 2 + o, place(y, ahead[o], c)) for o in (1, 0, 2)}
    core(t, 0)
    use(t)
    for o in (0, 2):
        to_z[o].wait_recv()
        core(place(y, behind[o], c), 9 + o)
    to_across.wait_recv()
    passed = {o: go(across, 5 + o // 2, place(y, ahead[o], c)) for o in (0, 2)}
    core(across, 8)
    to_z[1].wait_recv()
    far = go(place(y, behind[1], c), 7, across)
    core(place(y, behind[1], c), 10)
    use(place(y, behind[0], c))
    use(place(y, behind[2], c))
    use(across)
    use(place(y, behind[1], c))
    for o in (0, 2):
        passed[o].wait_recv()
        core(place(1 - y, behind[o], c), 12 + o // 2)
        use(place(1 - y, behind[o], c))
    to_core[0][0].wait_recv()
    use(other)
    far.wait_recv()
    core(place(1 - y, behind[1], c), 14)
    use(place(1 - y, behind[1], c))
    sources = [
        place(y, behind[0], 1 - c),
        place(y, behind[2], 1 - c),
        place(1 - y, z, 1 - c),
        place(y, behind[1], 1 - c),
        place(1 - y, behind[0], 1 - c),
        place(1 - y, behind[2], 1 - c),
        place(1 - y, behind[1], 1 - c),
    ]
    for (copy, _), block in zip(to_core[1:], sources):
        copy.wait_recv()
        use(block)
    for copy in started:
        copy.wait_send()


def order(row, column, at0, at1, vocab):
    again = jnp.where((column == row) & (at0 < at1), 1.0, 0.0)
    once = 1.0 - jnp.max(again, axis=0, keepdims=True)
    floor = column - lax.rem(column, vocab)
    before = jnp.where((row >= floor) & (row < column), once, 0.0)
    return once, jnp.sum(before, axis=1, keepdims=True).astype(jnp.int32)


def lookup_kernel(ids_ref, start_ref, table_hbm, emb, table, all_ids, out_d, in_d, out_t, in_t, local, ids_send, ids_recv,
                  d_send, d_recv, t_send, t_recv, g_send, g_recv):
    groups, holders = in_d.shape[0], in_t.shape[0]
    steps, row_count = ids_ref.shape
    rows, vocab, width = steps * row_count, table.shape[0], table.shape[1]
    block = width // holders
    half = width // 2
    g, t = lax.axis_index("dp"), lax.axis_index("tensor")
    load = pltpu.make_async_copy(table_hbm, table, local.at[0])
    load.start()
    row = jnp.concatenate([ids_ref[s : s + 1] for s in range(steps)], axis=1)
    all_ids[g] = jnp.broadcast_to(row, (8, rows))
    others_d = [lax.rem(g + o, groups) for o in range(1, groups)]
    others_t = [lax.rem(t + o, holders) for o in range(1, holders)]
    greet([{"dp": d} for d in others_d] + [{"tensor": d} for d in others_t])
    moves = []
    for o, d in enumerate(others_d):
        moves.append(remote(all_ids.at[g], all_ids.at[g], ids_send.at[o], ids_recv.at[o], dp=d))
        moves[-1].start()

    start = start_ref[0:1, 0:1]
    column = jnp.broadcast_to(row, (8, rows)).astype(jnp.float32).T.astype(jnp.int32)[:, 0:1]
    at0 = lax.broadcasted_iota(jnp.int32, (rows, rows), 0)
    at1 = lax.broadcasted_iota(jnp.int32, (rows, rows), 1)

    slot = order(row, column, at0, at1, vocab)[1] - start
    holder = column // vocab
    from_t, from_g = lax.rem(holder, holders), holder // holders
    want = jnp.where((slot >= 0) & (slot < SLOTS), (from_t * groups + from_g) * SLOTS + slot, -1)
    candidates = holders * groups * SLOTS

    for copy in moves:
        copy.wait()

    ids_all = all_ids[0]
    at_g = lax.broadcasted_iota(jnp.int32, (8, rows), 0)
    for gg in range(1, groups):
        ids_all = jnp.where(at_g == gg, all_ids[gg], ids_all)
    columns = ids_all.astype(jnp.float32).T.astype(jnp.int32)
    base = (g * holders + t) * vocab
    at_v = lax.broadcasted_iota(jnp.int32, (rows, vocab), 1)
    pick_g = lax.broadcasted_iota(jnp.int32, (16, vocab), 0)
    held = jnp.zeros((16, vocab), jnp.float32)
    for gg in range(groups):
        asked = jnp.where(columns[:, gg : gg + 1] - base == at_v, 1.0, 0.0)
        held = jnp.where(pick_g == gg, jnp.max(asked, axis=0, keepdims=True), held)
    lower = jnp.where(
        lax.broadcasted_iota(jnp.int32, (vocab, vocab), 0) < lax.broadcasted_iota(jnp.int32, (vocab, vocab), 1),
        1.0,
        0.0,
    ).astype(jnp.bfloat16)
    rank = jnp.dot(held.astype(jnp.bfloat16), lower, preferred_element_type=jnp.float32).astype(jnp.int32) - start
    at_c = lax.broadcasted_iota(jnp.int32, (SLOTS, vocab), 0)
    chosen = jnp.concatenate(
        [
            jnp.where((rank[gg : gg + 1] == at_c) & (held[gg : gg + 1] > 0.5), 1.0, 0.0)
            for gg in range(groups)
        ],
        axis=0,
    ).astype(jnp.bfloat16)
    load.wait()
    step = 512
    for at in range(0, half, step):
        low = jnp.dot(chosen, table[:, at : at + step], preferred_element_type=jnp.float32)
        high = jnp.dot(chosen, table[:, half + at : half + at + step], preferred_element_type=jnp.float32)
        both = jnp.concatenate(
            [low.reshape(groups, SLOTS, step), high.reshape(groups, SLOTS, step)], axis=1
        )
        out_d[:, :, at : at + step] = both.astype(jnp.bfloat16)
    sent = []
    for o, d in enumerate(others_d):
        sent.append(remote(out_d.at[d], in_d.at[g], d_send.at[o], d_recv.at[o], dp=d))
        sent[-1].start()
    in_d[g] = out_d[g]
    select = jnp.where(
        want == lax.broadcasted_iota(jnp.int32, (rows, candidates), 1), 1.0, 0.0
    ).astype(jnp.bfloat16)
    permute = jnp.where(at1 == lax.rem(at0, steps) * row_count + at0 // steps, 1.0, 0.0).astype(jnp.bfloat16)
    select = jnp.dot(permute, select, preferred_element_type=jnp.float32).astype(jnp.bfloat16)
    for copy in sent:
        copy.wait()
    for o in range(holders):
        part, at = o // (holders // 2), (o % (holders // 2)) * block
        piece = in_d[:, :, at : at + block].astype(jnp.float32)[:, part * SLOTS : (part + 1) * SLOTS]
        out_t[o] = piece.reshape(groups * SLOTS, block).astype(jnp.bfloat16)
    sent = []
    for o, d in enumerate(others_t):
        sent.append(remote(out_t.at[d], in_t.at[t], t_send.at[o], t_recv.at[o], tensor=d))
        sent[-1].start()
    in_t[t] = out_t[t]
    for copy in sent:
        copy.wait()
    found = jnp.dot(select, in_t[...].reshape(candidates, block), preferred_element_type=jnp.float32)
    emb[t] = found.astype(jnp.bfloat16)
    gather_blocks(emb, t, g_send, g_recv)


def lookup(ids, table, groups, holders, start):
    rows = ids.shape[0] * ids.shape[1]
    vocab, width = table.shape
    block = width // holders
    bf16, dma = jnp.bfloat16, pltpu.SemaphoreType.DMA
    vmem, anywhere = pl.BlockSpec(memory_space=pltpu.VMEM), pl.BlockSpec(memory_space=pl.ANY)
    return pl.pallas_call(
        lookup_kernel,
        out_shape=jax.ShapeDtypeStruct((holders, rows, block), bf16),
        in_specs=[vmem, vmem, anywhere],
        out_specs=vmem,
        scratch_shapes=[
            pltpu.VMEM((vocab, width), bf16),
            pltpu.VMEM((groups, 8, rows), jnp.int32),
            pltpu.VMEM((groups, 2 * SLOTS, width // 2), bf16),
            pltpu.VMEM((groups, 2 * SLOTS, width // 2), bf16),
            pltpu.VMEM((holders, groups * SLOTS, block), bf16),
            pltpu.VMEM((holders, groups * SLOTS, block), bf16),
            dma((1,)),
            dma((groups - 1,)),
            dma((groups - 1,)),
            dma((groups - 1,)),
            dma((groups - 1,)),
            dma((holders - 1,)),
            dma((holders - 1,)),
            dma((holders - 1,)),
            dma((holders - 1,)),
        ],
        compiler_params=pltpu.CompilerParams(collective_id=1, has_side_effects=True, vmem_limit_bytes=40 * 2**20),
        name="lookup_round",
    )(ids, start, table)


def normalize(whole, gain, out):
    holders, rows, block = whole.shape
    squares = jnp.zeros((rows, block), jnp.float32)
    for k in range(holders):
        wide = whole[k].astype(jnp.float32)
        squares = squares + wide * wide
    scale = lax.rsqrt(jnp.sum(squares, axis=1, keepdims=True) / (holders * block) + epsilon)
    for k in range(holders):
        at = slice(k * block, (k + 1) * block)
        out[:, at] = (whole[k].astype(jnp.float32) * scale * gain[:, at]).astype(jnp.bfloat16)


def project_kernel(mixed, weight_hbm, emb, next_gain, stream, normed, whole, weight, out_c, in_c, kept, out_z, in_z, slab, out_y, in_y, local,
                   c_send, c_recv, z_send, z_recv, y_send, y_recv, g_send, g_recv):
    t = lax.axis_index("tensor")
    block = whole.shape[2]
    load = pltpu.make_async_copy(weight_hbm, weight, local.at[0])
    load.start()
    y, z, c, ahead, behind, place = tensor_near(t)
    other, across = place(y, z, 1 - c), place(1 - y, z, c)
    greet([{"tensor": other}, {"tensor": across}] + [{"tensor": place(y, zz, c)} for zz in ahead])

    load.wait()
    rows_in = mixed[...]

    def partial_of(k, cc):
        at = place(k % 2, k // 2, cc) * block
        return jnp.dot(rows_in, weight[:, pl.ds(pl.multiple_of(at, block), block)], preferred_element_type=jnp.float32)

    to_core = []
    for k in range(2 * Z):
        out_c[k] = partial_of(k, 1 - c).astype(jnp.bfloat16)
        to_core.append(remote(out_c.at[k], in_c.at[k], c_send.at[k], c_recv.at[k], tensor=other))
        to_core[-1].start()
    for k in range(2 * Z):
        kept[k // 2, k % 2] = partial_of(k, c)
    for k in range(2 * Z):
        to_core[k].wait_recv()
        total = kept[k // 2, k % 2] + in_c[k].astype(jnp.float32)
        kept[k // 2, k % 2] = total
        out_z[k // 2, k % 2] = total.astype(jnp.bfloat16)
    to_z = []
    for o in range(Z - 1):
        to_z.append(
            remote(out_z.at[ahead[o]], in_z.at[o], z_send.at[o], z_recv.at[o], tensor=place(y, ahead[o], c))
        )
        to_z[-1].start()
    total = kept[z]
    for o in range(Z - 1):
        to_z[o].wait_recv()
        total = total + in_z[o].astype(jnp.float32)
    slab[...] = total
    out_y[...] = slab[1 - y].astype(jnp.bfloat16)
    to_y = remote(out_y, in_y, y_send.at[0], y_recv.at[0], tensor=across)
    to_y.start()
    to_y.wait_recv()
    branch = slab[y] + in_y[...].astype(jnp.float32)
    mine = (emb[t].astype(jnp.float32) + branch).astype(jnp.bfloat16)
    stream[...] = mine
    whole[t] = mine
    gather_blocks(whole, t, g_send, g_recv)
    normalize(whole, next_gain, normed)
    for copy in to_core + to_z + [to_y]:
        copy.wait_send()


def project(mixed, weight, emb, next_gain):
    holders, rows, block = emb.shape
    bf16, f32, dma = jnp.bfloat16, jnp.float32, pltpu.SemaphoreType.DMA
    vmem, anywhere = pl.BlockSpec(memory_space=pltpu.VMEM), pl.BlockSpec(memory_space=pl.ANY)
    return pl.pallas_call(
        project_kernel,
        out_shape=(
            jax.ShapeDtypeStruct((rows, block), bf16),
            jax.ShapeDtypeStruct((rows, holders * block), bf16),
        ),
        in_specs=[vmem, anywhere, vmem, vmem],
        out_specs=(vmem, vmem),
        scratch_shapes=[
            pltpu.VMEM((holders, rows, block), bf16),
            pltpu.VMEM(weight.shape, bf16),
            pltpu.VMEM((2 * Z, rows, block), bf16),
            pltpu.VMEM((2 * Z, rows, block), bf16),
            pltpu.VMEM((Z, 2, rows, block), f32),
            pltpu.VMEM((Z, 2, rows, block), bf16),
            pltpu.VMEM((Z - 1, 2, rows, block), bf16),
            pltpu.VMEM((2, rows, block), f32),
            pltpu.VMEM((rows, block), bf16),
            pltpu.VMEM((rows, block), bf16),
            dma((1,)),
            dma((2 * Z,)),
            dma((2 * Z,)),
            dma((Z - 1,)),
            dma((Z - 1,)),
            dma((1,)),
            dma((1,)),
            dma((holders - 1,)),
            dma((holders - 1,)),
        ],
        compiler_params=pltpu.CompilerParams(
            collective_id=2, has_side_effects=True, vmem_limit_bytes=40 * 2**20
        ),
        name="project",
    )(mixed, weight, emb, next_gain)


def readout(p, per, heads, steps, query, state, read):
    rows = read.shape[1]
    base = pl.multiple_of(p * (per * steps), per * steps)
    for h in range(heads):
        turned = pltpu.roll(query[h], lax.rem(rows - base, rows), 1)
        outs = []
        for i in range(per):
            old = state[p * per + i, h]
            for s in range(steps):
                lane = i * steps + s
                outs.append(jnp.sum(old * turned[:, lane : lane + 1], axis=0, keepdims=True))
        read[h, pl.ds(base, per * steps)] = jnp.concatenate(outs, axis=0)


def update(p, per, heads, steps, key, state, decay, xrow):
    rows = xrow.shape[1]
    base = pl.multiple_of(p * (per * steps), per * steps)
    for h in range(heads):
        turned = pltpu.roll(key[h], lax.rem(rows - base, rows), 1)
        for i in range(per):
            now = state[p * per + i, h]
            for s in range(steps):
                lane = i * steps + s
                now = decay[h, pl.ds(base + lane, 1)] * now + xrow[h, pl.ds(base + lane, 1)] * turned[:, lane : lane + 1]
            state[p * per + i, h] = now


def mix(h, proj, raw, bias, log_rate, columns, head_size, state_size, key, query, xin, xrow, decay):
    rows, at = proj.shape[0], h * columns
    value = raw[:, h : h + 1] + bias[h]
    size = jnp.maximum(value, 0.0) + jnp.log1p(jnp.exp(-jnp.abs(value)))
    rate = jnp.exp(-size * jnp.exp(jnp.full((rows, 1), log_rate[h], jnp.float32)))
    entry = proj[:, at : at + head_size]
    xin[h] = entry
    xrow[h] = size * entry
    decay[h] = jnp.broadcast_to(rate, (rows, head_size))
    at += 2 * head_size
    turned = proj[:, at : at + 2 * state_size].T
    key[h] = turned[:state_size]
    query[h] = turned[state_size:]


def close(h, steps, proj, skip, ngain, columns, head_size, state_size, xin, xrow, decay, read, mixed):
    at = h * columns
    rows = proj.shape[0]
    both = proj[:, at + 2 * head_size : at + 2 * head_size + 2 * state_size]
    queries = both[:, state_size:]
    step = lax.rem(lax.broadcasted_iota(jnp.int32, (rows, 1), 0), steps)
    rates, entry = decay[h], xrow[h]
    reach = rates
    out = jnp.sum(both[:, :state_size] * queries, axis=1, keepdims=True) * entry
    for back in range(1, steps):
        keys = pltpu.roll(both, back, 0)[:, :state_size]
        old = jnp.sum(keys * queries, axis=1, keepdims=True) * pltpu.roll(entry, back, 0)
        out = jnp.where(step >= back, out + reach * old, out)
        reach = jnp.where(step >= back, reach * pltpu.roll(rates, back, 0), reach)
    out = out + reach * read[h]
    out = out + skip[h] * xin[h]
    gate = proj[:, at + head_size : at + 2 * head_size]
    out = out * (gate / (1.0 + jnp.exp(-gate)))
    out = out * lax.rsqrt(jnp.mean(out * out, axis=1, keepdims=True) + epsilon)
    out = out * ngain[:, h * head_size : (h + 1) * head_size]
    mixed[:, h * head_size : (h + 1) * head_size] = out.astype(jnp.bfloat16)


def mixer_kernel(heads, emb, gain, weight_hbm, dtw, bias, log_rate, skip, ngain, state_hbm, new_hbm, mixed, weight, state, nrm, proj,
                 key, query, xin, xrow, decay, read, w_sem, s_sem, n_sem):
    holders, rows, block = emb.shape
    row_count, _, state_size, head_size = state.shape
    columns = weight.shape[1] // heads
    steps = rows // row_count
    parts = w_sem.shape[0]
    depth = weight.shape[0] // parts
    chunks = s_sem.shape[0]
    per = row_count // chunks
    loads = []
    for p in range(parts):
        at = pl.ds(p * depth, depth)
        loads.append(pltpu.make_async_copy(weight_hbm.at[at], weight.at[at], w_sem.at[p]))
        loads[-1].start()
    for p in range(chunks):
        at = pl.ds(p * per, per)
        pltpu.make_async_copy(state_hbm.at[at], state.at[at], s_sem.at[p]).start()

    squares = jnp.zeros((rows, block), jnp.float32)
    for k in range(holders):
        wide = emb[k].astype(jnp.float32)
        squares = squares + wide * wide
    scale = lax.rsqrt(jnp.sum(squares, axis=1, keepdims=True) / (holders * block) + epsilon)
    for k in range(holders):
        nrm[:, k * block : (k + 1) * block] = (emb[k].astype(jnp.float32) * scale * gain[:, k * block : (k + 1) * block]).astype(jnp.bfloat16)
    narrow = dtw[...].astype(jnp.float32)
    narrow = jnp.concatenate([narrow, jnp.zeros((16 - heads, narrow.shape[1]), jnp.float32)], axis=0).astype(jnp.bfloat16)
    steps_raw = lax.dot_general(nrm[...], narrow, (((1,), (1,)), ((), ())), preferred_element_type=jnp.float32)
    for p in range(parts):
        loads[p].wait()
        part = jnp.dot(nrm[:, p * depth : (p + 1) * depth], weight[p * depth : (p + 1) * depth],
                       preferred_element_type=jnp.float32)
        proj[...] = part if p == 0 else proj[...] + part

    sizes = (columns, head_size, state_size)
    for h in range(heads):
        mix(h, proj, steps_raw, bias, log_rate, *sizes, key, query, xin, xrow, decay)

    def chunk(p, carry):
        at = pl.ds(p * per, per)
        pltpu.make_async_copy(state_hbm.at[at], state.at[at], s_sem.at[p]).wait()
        readout(p, per, heads, steps, query, state, read)
        update(p, per, heads, steps, key, state, decay, xrow)
        pltpu.make_async_copy(state.at[at], new_hbm.at[at], n_sem.at[p]).start()
        return carry

    lax.fori_loop(0, chunks, chunk, 0)
    for h in range(heads):
        close(h, steps, proj, skip, ngain, *sizes, xin, xrow, decay, read, mixed)
    for p in range(chunks):
        at = pl.ds(p * per, per)
        pltpu.make_async_copy(state.at[at], new_hbm.at[at], n_sem.at[p]).wait()


def mixer(emb, gain, weight, dtw, bias, log_rate, skip, ngain, state):
    holders, rows, block = emb.shape
    row_count, heads, state_size, head_size = state.shape
    bf16, f32, dma = jnp.bfloat16, jnp.float32, pltpu.SemaphoreType.DMA
    vmem, anywhere = pl.BlockSpec(memory_space=pltpu.VMEM), pl.BlockSpec(memory_space=pl.ANY)
    smem = pl.BlockSpec(memory_space=pltpu.SMEM)
    return pl.pallas_call(
        functools.partial(mixer_kernel, heads),
        out_shape=(
            jax.ShapeDtypeStruct(state.shape, f32),
            jax.ShapeDtypeStruct((rows, heads * head_size), bf16),
        ),
        in_specs=[vmem, vmem, anywhere, vmem, smem, smem, smem, vmem, anywhere],
        out_specs=(anywhere, vmem),
        scratch_shapes=[
            pltpu.VMEM(weight.shape, bf16),
            pltpu.VMEM(state.shape, f32),
            pltpu.VMEM((rows, holders * block), bf16),
            pltpu.VMEM((rows, weight.shape[1]), f32),
            pltpu.VMEM((heads, state_size, rows), f32),
            pltpu.VMEM((heads, state_size, rows), f32),
            pltpu.VMEM((heads, rows, head_size), f32),
            pltpu.VMEM((heads, rows, head_size), f32),
            pltpu.VMEM((heads, rows, head_size), f32),
            pltpu.VMEM((heads, rows, head_size), f32),
            dma((4,)),
            dma((8,)),
            dma((8,)),
        ],
        compiler_params=pltpu.CompilerParams(vmem_limit_bytes=40 * 2**20),
        name="mixer",
    )(emb, gain, weight, dtw, bias, log_rate, skip, ngain, state)


def fused_kernel(heads, ids_in, table_hbm, trainer_hbm, gain, weight_hbm, dtw, bias, log_rate, skip, ngain,
                 state_hbm, oweight_hbm, next_gain, head_map, new_hbm, stream, normed, gathered, swap, need, table,
                 trainer, weight, state, oweight, all_ids, out_d, in_d, out_t, in_t, out_r, in_r, emb, whole,
                 swap_out, proj, narrow, raw, key, query, xin, xrow, decay, read, mixed, out_c, in_c, kept, out_z,
                 in_z, slab, out_y, in_y, l_sem, w_sem, s_sem, n_sem, i_send, i_recv, d_send, d_recv, t_send,
                 t_recv, r_send, r_recv, e_send, e_recv, a_send, a_recv, x_send, x_recv, c_send, c_recv, z_send,
                 z_recv, y_send, y_recv, g_send, g_recv):
    bf16, f32 = jnp.bfloat16, jnp.float32
    groups, holders = in_d.shape[0], in_t.shape[0]
    vocab, width = table.shape
    rows, block = emb.shape[1], emb.shape[2]
    half = width // 2
    row_count, _, state_size, head_size = state.shape
    steps = rows // row_count
    trows = trainer.shape[0]
    g, t = lax.axis_index("dp"), lax.axis_index("tensor")
    y, z, c, ahead, behind, place = tensor_near(t)
    other, across = place(y, z, 1 - c), place(1 - y, z, c)
    x, low = g // 2, lax.rem(g, 2)
    beside = x * 2 + 1 - low
    x_ahead = [lax.rem(x + o, X) * 2 + low for o in range(1, X)]
    x_behind = [lax.rem(x + X - o, X) * 2 + low for o in range(1, X)]

    load_table = pltpu.make_async_copy(table_hbm, table, l_sem.at[0])
    load_table.start()
    load_trainer = pltpu.make_async_copy(trainer_hbm, trainer, l_sem.at[1])
    load_trainer.start()
    ids2 = ids_in[...]
    row = jnp.concatenate([ids2[s : s + 1] for s in range(steps)], axis=1)
    all_ids[g] = jnp.broadcast_to(row, (8, rows))
    others_d = [lax.rem(g + o, groups) for o in range(1, groups)]
    others_t = [lax.rem(t + o, holders) for o in range(1, holders)]
    greet([{"dp": d} for d in others_d] + [{"tensor": d} for d in others_t])
    moves = []
    for o, d in enumerate(others_d):
        moves.append(remote(all_ids.at[g], all_ids.at[g], i_send.at[o], i_recv.at[o], dp=d))
        moves[-1].start()

    load_oweight = pltpu.make_async_copy(oweight_hbm, oweight, l_sem.at[2])
    loads_w = [
        pltpu.make_async_copy(weight_hbm.at[pl.ds(k * block, block)], weight.at[k], w_sem.at[k])
        for k in range(holders)
    ]
    chunks = s_sem.shape[0]
    per = row_count // chunks

    def old_state(p):
        at = pl.ds(p * per, per)
        return pltpu.make_async_copy(state_hbm.at[at], state.at[at], s_sem.at[p])

    def fresh_state(p):
        at = pl.ds(p * per, per)
        return pltpu.make_async_copy(state.at[at], new_hbm.at[at], n_sem.at[p])

    load_trainer.wait()
    for o in range(holders):
        swap_out[o] = trainer[:, o * block : (o + 1) * block].astype(bf16)
    swaps = []
    for o, d in enumerate(others_t):
        swaps.append(remote(swap_out.at[d], gathered.at[g, t], a_send.at[o], a_recv.at[o], tensor=d))
        swaps[-1].start()
    gathered[g, t] = swap_out[t]
    for copy in loads_w + [load_oweight]:
        copy.start()
    for p in range(chunks):
        old_state(p).start()

    at0 = lax.broadcasted_iota(jnp.int32, (rows, rows), 0)
    at1 = lax.broadcasted_iota(jnp.int32, (rows, rows), 1)

    def turn(column):
        return jnp.broadcast_to(column.astype(f32), (rows, rows)).T[0:1].astype(jnp.int32)

    def places(row, column):
        once, slot = order(row, column, at0, at1, vocab)
        fits = jnp.where(turn(slot) < SLOTS, once, 0.0)
        column_t, row_t = lax.rem(column // vocab, holders), lax.rem(row // vocab, holders)
        before = jnp.where((row_t == column_t) & (row < column), fits, 0.0)
        return once, slot, jnp.sum(before, axis=1, keepdims=True).astype(jnp.int32)

    column = jnp.broadcast_to(row, (8, rows)).astype(f32).T.astype(jnp.int32)[:, 0:1]
    once, slot, index = places(row, column)
    from_t, from_g = lax.rem(column // vocab, holders), column // (vocab * holders)
    comes = (slot < SLOTS) & (index < WIDE)
    want = jnp.where(comes, from_t * WIDE + index, -1)
    select = jnp.where(want == lax.broadcasted_iota(jnp.int32, (rows, holders * WIDE), 1), 1.0, 0.0).astype(bf16)
    permute = jnp.where(at1 == lax.rem(at0, steps) * row_count + at0 // steps, 1.0, 0.0).astype(bf16)
    select = jnp.dot(permute, select, preferred_element_type=f32).astype(bf16)
    index_row = turn(jnp.where((from_t == t) & comes, index, -1))
    lift = jnp.where(
        (lax.broadcasted_iota(jnp.int32, (WIDE, rows), 0) == index_row) & (once > 0.5), 1.0, 0.0
    ).astype(bf16)
    spot = jnp.where(slot < SLOTS, from_g * (2 * SLOTS) + slot, -2 * SLOTS * groups)
    take_low = jnp.dot(lift, jnp.where(spot == at1, 1.0, 0.0).astype(bf16), preferred_element_type=f32).astype(bf16)
    take_high = jnp.dot(
        lift, jnp.where(spot + SLOTS == at1, 1.0, 0.0).astype(bf16), preferred_element_type=f32
    ).astype(bf16)
    lower = jnp.where(
        lax.broadcasted_iota(jnp.int32, (vocab, vocab), 0) < lax.broadcasted_iota(jnp.int32, (vocab, vocab), 1),
        1.0,
        0.0,
    ).astype(bf16)

    for copy in moves:
        copy.wait()
    ids_all = all_ids[0]
    at_g = lax.broadcasted_iota(jnp.int32, (8, rows), 0)
    for gg in range(1, groups):
        ids_all = jnp.where(at_g == gg, all_ids[gg], ids_all)
    columns = ids_all.astype(f32).T.astype(jnp.int32)
    base = (g * holders + t) * vocab
    at_v = lax.broadcasted_iota(jnp.int32, (rows, vocab), 1)
    pick_g = lax.broadcasted_iota(jnp.int32, (16, vocab), 0)
    held = jnp.zeros((16, vocab), f32)
    for gg in range(groups):
        asked = jnp.where(columns[:, gg : gg + 1] - base == at_v, 1.0, 0.0)
        held = jnp.where(pick_g == gg, jnp.max(asked, axis=0, keepdims=True), held)
    rank = jnp.dot(held.astype(bf16), lower, preferred_element_type=f32).astype(jnp.int32)
    at_c = lax.broadcasted_iota(jnp.int32, (SLOTS, vocab), 0)
    chosen = jnp.concatenate(
        [
            jnp.where((rank[gg : gg + 1] == at_c) & (held[gg : gg + 1] > 0.5), 1.0, 0.0)
            for gg in range(groups)
        ],
        axis=0,
    ).astype(bf16)
    load_table.wait()
    step = 512
    for at in range(0, half, step):
        left = jnp.dot(chosen, table[:, at : at + step], preferred_element_type=f32)
        right = jnp.dot(chosen, table[:, half + at : half + at + step], preferred_element_type=f32)
        both = jnp.concatenate(
            [left.reshape(groups, SLOTS, step), right.reshape(groups, SLOTS, step)], axis=1
        )
        out_d[:, :, at : at + step] = both.astype(bf16)
    sent = []
    for o, d in enumerate(others_d):
        sent.append(remote(out_d.at[d], in_d.at[g], d_send.at[o], d_recv.at[o], dp=d))
        sent[-1].start()
    in_d[g] = out_d[g]

    most = jnp.zeros((1, 1), jnp.int32)
    over = jnp.zeros((1, 1), jnp.int32)
    for gg in range(groups):
        _, slots, indices = places(all_ids[gg][0:1], columns[:, gg : gg + 1])
        most = jnp.maximum(most, jnp.max(slots, axis=0, keepdims=True))
        over = jnp.maximum(over, jnp.max(indices, axis=0, keepdims=True))
    todo = jnp.where((most >= SLOTS) | (over >= WIDE), most + 1, 0)
    need[0, 0] = todo[0, 0]
    units = heads * head_size
    maps = jnp.concatenate(
        [head_map[...].astype(f32), jnp.zeros((8 - heads, head_size), f32)], axis=0
    ).T.astype(jnp.int32)
    at_u = lax.broadcasted_iota(jnp.int32, (head_size, units), 1)
    for h in range(heads):
        swap[h * head_size : (h + 1) * head_size] = jnp.where(
            maps[:, h : h + 1] + h * head_size == at_u, 1.0, 0.0
        ).astype(bf16)
    for k in range(holders):
        thin = dtw[:, k * block : (k + 1) * block].astype(f32)
        narrow[k] = jnp.concatenate([thin, jnp.zeros((16 - heads, block), f32)], axis=0).astype(bf16)
    proj[...] = jnp.zeros_like(proj)
    raw[...] = jnp.zeros_like(raw)

    for copy in sent:
        copy.wait()
    arrived = in_d[...].reshape(groups * 2 * SLOTS, half)
    total = jnp.zeros((WIDE, block), f32)
    for part, take in enumerate((take_low, take_high)):
        for k in range(holders // 2):
            piece = jnp.dot(take, arrived[:, k * block : (k + 1) * block], preferred_element_type=f32)
            out_r[part * (holders // 2) + k] = piece.astype(bf16)
            total = total + piece * piece
    scale = lax.rsqrt(jnp.sum(total, axis=1, keepdims=True) / width + epsilon)
    for k in range(holders):
        scaled = out_r[k].astype(f32) * scale * gain[:, k * block : (k + 1) * block]
        out_t[k] = scaled.astype(bf16)
    sent = []
    for o, d in enumerate(others_t):
        sent.append(remote(out_t.at[d], in_t.at[t], t_send.at[o], t_recv.at[o], tensor=d))
        sent[-1].start()
    in_t[t] = out_t[t]

    shared = []

    def share(block_at, role, to):
        copy = remote(gathered.at[block_at], gathered.at[block_at], x_send.at[role], x_recv.at[role], dp=to)
        copy.start()
        shared.append(copy)
        return copy

    for copy in swaps:
        copy.wait()
    to_x = [share(g, 1 + o, x_ahead[o]) for o in range(X - 1)]

    for copy in sent:
        copy.wait()
    found = jnp.dot(select, in_t[...].reshape(holders * WIDE, block), preferred_element_type=f32)
    emb[t] = found.astype(bf16)

    def project_in(k):
        proj[...] += jnp.dot(emb[k], weight[k], preferred_element_type=f32)
        raw[...] += lax.dot_general(emb[k], narrow[k], (((1,), (1,)), ((), ())), preferred_element_type=f32)

    for copy in loads_w:
        copy.wait()
    gather_blocks(emb, t, e_send, e_recv, project_in)
    residual = []
    for o, d in enumerate(others_t):
        residual.append(remote(out_r.at[d], in_r.at[t], r_send.at[o], r_recv.at[o], tensor=d))
        residual[-1].start()
    in_r[t] = out_r[t]
    to_beside = share(g, 0, beside)
    sizes = (weight.shape[2] // heads, head_size, state_size)
    for h in range(heads):
        mix(h, proj, raw, bias, log_rate, *sizes, key, query, xin, xrow, decay)

    def look(p, carry):
        old_state(p).wait()
        readout(p, per, heads, steps, query, state, read)
        return carry

    lax.fori_loop(0, chunks, look, 0)
    for h in range(heads):
        close(h, steps, proj, skip, ngain, *sizes, xin, xrow, decay, read, mixed)

    load_oweight.wait()
    rows_in = mixed[...]

    def partial_of(k, cc):
        at = place(k % 2, k // 2, cc) * block
        return jnp.dot(rows_in, oweight[:, pl.ds(pl.multiple_of(at, block), block)], preferred_element_type=f32)

    to_core = []
    for k in range(2 * Z):
        out_c[k] = partial_of(k, 1 - c).astype(bf16)
        to_core.append(remote(out_c.at[k], in_c.at[k], c_send.at[k], c_recv.at[k], tensor=other))
        to_core[-1].start()
    for k in range(2 * Z):
        kept[k // 2, k % 2] = partial_of(k, c)
    for k in range(2 * Z):
        to_core[k].wait_recv()
        total = kept[k // 2, k % 2] + in_c[k].astype(f32)
        kept[k // 2, k % 2] = total
        out_z[k // 2, k % 2] = total.astype(bf16)
    to_z = []
    for o in range(Z - 1):
        to_z.append(
            remote(out_z.at[ahead[o]], in_z.at[o], z_send.at[o], z_recv.at[o], tensor=place(y, ahead[o], c))
        )
        to_z[-1].start()

    def move_on(p, carry):
        update(p, per, heads, steps, key, state, decay, xrow)
        fresh_state(p).start()
        return carry

    lax.fori_loop(0, chunks // 2, move_on, 0)
    to_beside.wait_recv()
    passed = [share(beside, X + o, x_ahead[o]) for o in range(X - 1)]
    lax.fori_loop(chunks // 2, chunks, move_on, 0)
    for copy in residual:
        copy.wait()
    embedded = jnp.dot(select, in_r[...].reshape(holders * WIDE, block), preferred_element_type=f32)
    total = kept[z]
    for o in range(Z - 1):
        to_z[o].wait_recv()
        total = total + in_z[o].astype(f32)
    slab[...] = total
    out_y[...] = slab[1 - y].astype(bf16)
    to_y = remote(out_y, in_y, y_send.at[0], y_recv.at[0], tensor=across)
    to_y.start()
    to_y.wait_recv()
    branch = slab[y] + in_y[...].astype(f32)
    mine = (embedded + branch).astype(bf16)
    stream[...] = mine
    whole[t] = mine

    gather_blocks(whole, t, g_send, g_recv)
    normalize(whole, next_gain, normed)
    for copy in to_x + passed:
        copy.wait_recv()
    for copy in to_core + to_z + [to_y] + shared:
        copy.wait_send()
    for p in range(chunks):
        fresh_state(p).wait()


def fused(ids, table, trainer, gain, weight, dtw, bias, log_rate, skip, ngain, state, oweight, next_gain, head_map,
          groups, holders):
    row_count, heads, state_size, head_size = state.shape
    rows = ids.shape[0] * ids.shape[1]
    vocab, width = table.shape
    block = width // holders
    trows = trainer.shape[0]
    units = heads * head_size
    columns = weight.shape[1]
    bf16, f32, dma = jnp.bfloat16, jnp.float32, pltpu.SemaphoreType.DMA
    vmem, anywhere = pl.BlockSpec(memory_space=pltpu.VMEM), pl.BlockSpec(memory_space=pl.ANY)
    smem = pl.BlockSpec(memory_space=pltpu.SMEM)
    buffers = [
        ((vocab, width), bf16),
        (trainer.shape, f32),
        ((holders, block, columns), bf16),
        (state.shape, f32),
        (oweight.shape, bf16),
        ((groups, 8, rows), jnp.int32),
        ((groups, 2 * SLOTS, width // 2), bf16),
        ((groups, 2 * SLOTS, width // 2), bf16),
        ((holders, WIDE, block), bf16),
        ((holders, WIDE, block), bf16),
        ((holders, WIDE, block), bf16),
        ((holders, WIDE, block), bf16),
        ((holders, rows, block), bf16),
        ((holders, rows, block), bf16),
        ((holders, trows, block), bf16),
        ((rows, columns), f32),
        ((holders, 16, block), bf16),
        ((rows, 16), f32),
        ((heads, state_size, rows), f32),
        ((heads, state_size, rows), f32),
        ((heads, rows, head_size), f32),
        ((heads, rows, head_size), f32),
        ((heads, rows, head_size), f32),
        ((heads, rows, head_size), f32),
        ((rows, units), bf16),
        ((2 * Z, rows, block), bf16),
        ((2 * Z, rows, block), bf16),
        ((Z, 2, rows, block), f32),
        ((Z, 2, rows, block), bf16),
        ((Z - 1, 2, rows, block), bf16),
        ((2, rows, block), f32),
        ((rows, block), bf16),
        ((rows, block), bf16),
    ]
    semaphores = [3, holders, 8, 8]
    for count in (groups - 1, groups - 1, holders - 1, holders - 1, holders - 1, holders - 1, 2 * X - 1, 2 * Z, Z - 1, 1):
        semaphores += [count, count]
    semaphores += [holders - 1, holders - 1]
    return pl.pallas_call(
        functools.partial(fused_kernel, heads),
        out_shape=(
            jax.ShapeDtypeStruct(state.shape, f32),
            jax.ShapeDtypeStruct((rows, block), bf16),
            jax.ShapeDtypeStruct((rows, width), bf16),
            jax.ShapeDtypeStruct((groups, holders, trows, block), bf16),
            jax.ShapeDtypeStruct((units, units), bf16),
            jax.ShapeDtypeStruct((1, 1), jnp.int32),
        ),
        in_specs=[vmem, anywhere, anywhere, vmem, anywhere, vmem, smem, smem, smem, vmem, anywhere, anywhere, vmem, vmem],
        out_specs=(anywhere, vmem, vmem, vmem, vmem, smem),
        scratch_shapes=[pltpu.VMEM(*buffer) for buffer in buffers] + [dma((count,)) for count in semaphores],
        compiler_params=pltpu.CompilerParams(
            collective_id=0, has_side_effects=True, vmem_limit_bytes=60 * 2**20
        ),
        name="fused",
    )(ids, table, trainer, gain, weight, dtw, bias, log_rate, skip, ngain, state, oweight, next_gain, head_map)


def per_device(
    token_ids,
    embed_table,
    in_gain,
    in_weight,
    dt_weight,
    dt_bias,
    a_log,
    d_skip,
    norm_gain,
    out_weight,
    next_gain,
    ssm_state,
    trainer_weight,
    head_map,
):
    row_count, step_count = token_ids.shape
    width = embed_table.shape[1]
    holders = lax.axis_size("tensor")
    groups = lax.axis_size("dp")
    rows = row_count * step_count
    state = ssm_state.swapaxes(2, 3)
    gain, ngain, ngain_next = in_gain.reshape(1, -1), norm_gain.reshape(1, -1), next_gain.reshape(1, -1)
    mix = (in_weight, dt_weight.T, dt_bias, a_log, d_skip, ngain, state)
    now, stream, normed, gathered, swap, need = fused(
        token_ids.T, embed_table, trainer_weight, gain, *mix, out_weight, ngain_next, head_map, groups, holders
    )

    def again(carry):
        todo = carry[0]

        def more(inner):
            done, held = inner
            return done + SLOTS, held + lookup(token_ids.T, embed_table, groups, holders, jnp.full((8, 128), done, jnp.int32))

        empty = jnp.zeros((holders, rows, width // holders), jnp.bfloat16)
        _, emb = lax.while_loop(lambda inner: inner[0] < todo, more, (jnp.int32(0), empty))
        now, mixed = mixer(emb, gain, *mix)
        stream, normed = project(mixed, out_weight, emb, ngain_next)
        return jnp.int32(0), now, stream, normed

    _, now, stream, normed = lax.while_loop(
        lambda carry: carry[0] > 0, again, (need.reshape(()), now, stream, normed)
    )
    relaid = lax.dot_general(
        swap,
        gathered.reshape(width, swap.shape[1]),
        (((1,), (1,)), ((), ())),
        preferred_element_type=jnp.float32,
    )
    return (
        now.swapaxes(2, 3),
        stream.reshape(row_count, step_count, -1),
        normed.reshape(row_count, step_count, width),
        relaid,
    )


def solution(mesh):
    placed = (
        P("dp", None),
        P(("dp", "tensor"), None),
        P(),
        P(None, "tensor"),
        P(None, "tensor"),
        P("tensor"),
        P("tensor"),
        P("tensor"),
        P("tensor"),
        P("tensor", None),
        P(),
        P("dp", "tensor", None, None),
        P(("dp", "tensor"), None),
        P("tensor", None),
    )
    return jax.shard_map(
        per_device,
        mesh=mesh,
        in_specs=placed,
        out_specs=(
            P("dp", "tensor", None, None),
            P("dp", None, "tensor"),
            P("dp", None, None),
            P("tensor", None),
        ),
        check_vma=False,
    )
```

time: 104 us -> 87.5 us (0.84)
  Pallas kernels: 85.3 us -> 75 us
  local copies, waits for them, and re-layouts: 11.8 us -> 6.08 us
  other arithmetic: 2.08 us -> 0 us
  matrix products: 2.77 us -> 4.5 us
    pallas_call x3 -> x1, Pallas kernels: 85.3 us -> 75 us  [fused(): pl.pallas_call(functools.partial(fused_kernel, heads), out_shape=(jax.Sha...]
    unnamed x12 -> x23, local copies, waits for them, and re-layouts: 6.02 us -> 2.06 us
    dot_general x1, matrix products: 2.77 us -> 4.5 us  [per_device(): lax.dot_general(swap, gathered.reshape(width, swap.shape[1]), (((1,), (1,...]
    slice x1 -> x0, local copies, waits for them, and re-layouts: 1.18 us -> none  [per_device(): need[0, 0]]
    reshape x4 -> x2, local copies, waits for them, and re-layouts: 3.29 us -> 4.02 us  [the longest x1 2.52 us: per_device(): normed.reshape(row_count, step_count, width)]
where the time goes in v3:
time: 87.5 us; the launch traced here: 87.3 us
  Pallas kernels  75 us (86%)
  local copies, waits for them, and re-layouts  6.08 us (7%)
  matrix products  4.5 us (5%)
  loops' own time  0.9 us (1%)
    pallas_call x1, Pallas kernels, fused(): pl.pallas_call(functools.partial(fused_kernel, heads), out_shape=(jax.Sha...  75 us
    dot_general x1, matrix products, per_device(): lax.dot_general(swap, gathered.reshape(width, swap.shape[1]), (((1,), (1,...  4.5 us
    reshape x1, local copies, waits for them, and re-layouts, per_device(): normed.reshape(row_count, step_count, width)  2.52 us
    unnamed x23, local copies, waits for them, and re-layouts  2.06 us

profile of v3, /device:TPU:1, one launch (start us, length us, event | category | flops | bytes accessed | tf_op | source)
XLA Modules:
  0.0 87.3 jit_solution(5380791617438984023)
XLA Ops:
  0.6 0.0 copy-start
  0.6 0.0 copy-start.2
  0.7 0.0 copy-start.3
  0.7 0.0 copy-start.4
  0.7 0.0 copy-start.5
  0.7 0.0 copy-start.7
  0.7 0.0 copy-start.8
  0.7 0.0 copy-start.9
  0.7 0.0 copy-start.10
  0.7 75.0 %fused.1 = (f32[64,2,64,128]{3,2,1,0:T(8,128)}, bf16[128,256]{1,0:T(8,128)(2,1)}, bf16[128,4096]{1,0:T(8,128)(2,1)}, bf16[8,16,32,256]{3,2,1,0:T(8,128)(2,1)}, bf16[256,256]{1,0:T(8,128)(2,1)}, /*index=5*/s32[1,1]{1,0:T(1,128)}) custom-call(s32[2,64]{1,0:T(2,128)} %bitcast.18, bf16[512,4096]{1,0:T(8,128)(2,1)} %table_hbm.1, f32[32,4096]{1,0:T(8,128)} %trainer_hbm.1, ...), custom_call_target="tpu_custom_call" | custom-call | tf_op jit(solution)/shard_map/fused/pallas_call | solution.py:836
  75.8 0.0 copy-done
  75.8 0.0 copy-done.2
  75.8 0.0 copy-done.3
  75.8 0.0 copy-done.4
  75.8 0.0 copy-done.5
  75.8 0.0 copy-done.7
  75.8 0.0 copy-done.8
  75.8 0.0 copy-done.9
  75.9 0.9 %while.22 = (s32[]{:T(128)}, f32[64,2,64,128]{3,2,1,0:T(8,128)}, bf16[128,256]{1,0:T(8,128)(2,1)}, bf16[128,4096]{1,0:T(8,128)(2,1)}, s32[64,2]{0,1:T(2,128)S(1)...) while((s32[]{:T(128)}, f32[64,2,64,128]{3,2,1,0:T(8,128)}, ...), condition=%region_3.0_spmd, body=%region_0.0_spmd | while | flops 524291 | bytes 4198700 | solution.py:897
  76.8 1.5 %reshape.33 = bf16[64,2,256]{2,1,0:T(2,128)(2,1)} reshape(bf16[128,256]{1,0:T(8,128)(2,1)} %get-tuple-element.299) | data formatting | bytes 131072 | tf_op jit(solution)/shard_map/reshape | solution.py:908
  78.3 2.5 %reshape.34 = bf16[64,2,4096]{2,1,0:T(2,128)(2,1)} reshape(bf16[128,4096]{1,0:T(8,128)(2,1)} %get-tuple-element.300) | data formatting | bytes 2097152 | tf_op jit(solution)/shard_map/reshape | solution.py:909
  80.8 4.5 %fusion = f32[256,4096]{1,0:T(8,128)} fusion(bf16[256,256]{1,0:T(8,128)(2,1)S(1)} %copy-done.6, bf16[4096,256]{1,0:T(8,128)(2,1)} %bitcast.17), kind=kOutput, calls=%fused_computation | convolution fusion | flops 536870912 | bytes 6422528 | tf_op jit(solution)/shard_map/dot_general | solution.py:900
  85.3 0.0 copy-done.1
  85.3 2.0 %copy.39 = f32[64,2,128,64]{2,3,1,0:T(8,128)} copy(f32[64,2,128,64]{2,3,1,0:T(8,128)S(1)} %bitcast.16) | data formatting | bytes 8388608
  (4 shorter events, 0.0 us)
Async XLA Ops:
  0.6 75.1 %copy-start = (bf16[256,4096]{1,0:T(8,128)(2,1)S(1)}, bf16[256,4096]{1,0:T(8,128)(2,1)}, u32[]{:S(2)}) copy-start(bf16[256,4096]{1,0:T(8,128)(2,1)} %oweight_hbm.1) | copy-start | bytes 6291460
  0.6 75.1 %copy-start.2 = (s32[64,2]{0,1:T(2,128)S(1)}, s32[64,2]{0,1:T(2,128)}, u32[]{:S(2)}) copy-start(s32[64,2]{0,1:T(2,128)} %param.18) | copy-start | bytes 1540
  0.7 75.1 %copy-start.3 = (f32[4096]{0:T(1024)S(1)}, f32[4096]{0:T(1024)}, u32[]{:S(2)}) copy-start(f32[4096]{0:T(1024)} %param.20) | copy-start | bytes 49156
  0.7 75.1 %copy-start.4 = (bf16[4096,2]{0,1:T(2,128)(2,1)S(1)}, bf16[4096,2]{0,1:T(2,128)(2,1)}, u32[]{:S(2)}) copy-start(bf16[4096,2]{0,1:T(2,128)(2,1)} %param.22) | copy-start | bytes 49156
  0.7 75.1 %copy-start.5 = (f32[4096]{0:T(1024)S(1)}, f32[4096]{0:T(1024)}, u32[]{:S(2)}) copy-start(f32[4096]{0:T(1024)} %param.28) | copy-start | bytes 49156
  0.7 75.1 %copy-start.7 = (f32[256]{0:T(256)S(1)}, f32[256]{0:T(256)}, u32[]{:S(2)}) copy-start(f32[256]{0:T(256)} %param.26) | copy-start | bytes 3076
  0.7 75.1 %copy-start.8 = (f32[2]{0:T(128)S(1)}, f32[2]{0:T(128)}, u32[]{:S(2)}) copy-start(f32[2]{0:T(128)} %bias.1) | copy-start | bytes 28
  0.7 75.1 %copy-start.9 = (f32[2]{0:T(128)S(1)}, f32[2]{0:T(128)}, u32[]{:S(2)}) copy-start(f32[2]{0:T(128)} %log_rate.1) | copy-start | bytes 28
  0.7 75.1 %copy-start.10 = (f32[2]{0:T(128)S(1)}, f32[2]{0:T(128)}, u32[]{:S(2)}) copy-start(f32[2]{0:T(128)} %skip.1) | copy-start | bytes 28
  75.8 4.9 %copy-start.6 = (bf16[256,256]{1,0:T(8,128)(2,1)S(1)}, bf16[256,256]{1,0:T(8,128)(2,1)}, u32[]{:S(2)}) copy-start(bf16[256,256]{1,0:T(8,128)(2,1)} %get-tuple-element.130) | copy-start | bytes 393220
  80.8 4.5 %copy-start.1 = (f32[64,2,64,128]{3,2,1,0:T(8,128)S(1)}, f32[64,2,64,128]{3,2,1,0:T(8,128)}, u32[]{:S(2)}) copy-start(f32[64,2,64,128]{3,2,1,0:T(8,128)} %get-tuple-element.298) | copy-start | bytes 12582916

commit v4 on v3

--- a/solution.py
+++ b/solution.py
@@ -40,59 +40,55 @@
     return y, z, c, ahead, behind, place
 
 
-def gather_blocks(buf, t, send, recv, use=lambda block: None):
+def spot(t):
+    return lax.rem(t, 2) * (2 * Z) + t // 2 if not isinstance(t, int) else t % 2 * (2 * Z) + t // 2
+
+
+def farthest_first(t):
+    y, z, c, ahead, _, place = tensor_near(t)
+    chips = [(1 - y, ahead[1]), (1 - y, ahead[0]), (1 - y, ahead[2]), (1 - y, z)]
+    chips += [(y, ahead[1]), (y, ahead[0]), (y, ahead[2])]
+    return [place(yy, zz, cc) for yy, zz in chips for cc in (c, 1 - c)] + [place(y, z, 1 - c)]
+
+
+def gather_blocks(buf, t, send, recv, use=lambda at, position: None):
     y, z, c, ahead, behind, place = tensor_near(t)
-    other, across = place(y, z, 1 - c), place(1 - y, z, c)
-    started, to_core = [], []
-
-    def go(block, role, to):
-        copy = remote(buf.at[block], buf.at[block], send.at[role], recv.at[role], tensor=to)
+    other = place(y, z, 1 - c)
+    to = [(1 - y, ahead[1]), (1 - y, ahead[0]), (1 - y, ahead[2]), (1 - y, z), (y, ahead[1]), (y, ahead[0]), (y, ahead[2])]
+    own = spot(t)
+    sent = []
+    for role, (yy, zz) in enumerate(to):
+        sent.append(remote(buf.at[own], buf.at[own], send.at[role], recv.at[role], tensor=place(yy, zz, c)))
+        sent[-1].start()
+
+    def core(yy, role):
+        at = pl.ds((c * 2 + yy) * Z, Z)
+        copy = remote(buf.at[at], buf.at[at], send.at[role], recv.at[role], tensor=other)
         copy.start()
-        started.append(copy)
         return copy
 
-    def core(block, role):
-        to_core.append((go(block, role, other), role))
-
-    to_across = go(t, 1, across)
-    to_z = {o: go(t, 2 + o, place(y, ahead[o], c)) for o in (1, 0, 2)}
-    core(t, 0)
-    use(t)
-    for o in (0, 2):
-        to_z[o].wait_recv()
-        core(place(y, behind[o], c), 9 + o)
-    to_across.wait_recv()
-    passed = {o: go(across, 5 + o // 2, place(y, ahead[o], c)) for o in (0, 2)}
-    core(across, 8)
-    to_z[1].wait_recv()
-    far = go(place(y, behind[1], c), 7, across)
-    core(place(y, behind[1], c), 10)
-    use(place(y, behind[0], c))
-    use(place(y, behind[2], c))
-    use(across)
-    use(place(y, behind[1], c))
-    for o in (0, 2):
-        passed[o].wait_recv()
-        core(place(1 - y, behind[o], c), 12 + o // 2)
-        use(place(1 - y, behind[o], c))
-    to_core[0][0].wait_recv()
-    use(other)
+    def used(yy, zz, cc):
+        position = place(yy, zz, cc)
+        use(spot(position), position)
+
+    used(y, z, c)
+    for role in (5, 6, 4):
+        sent[role].wait_recv()
+    near = core(y, 7)
+    for zz in behind:
+        used(y, zz, c)
+    for role in (3, 1, 2, 0):
+        sent[role].wait_recv()
+    far = core(1 - y, 8)
+    for zz in [z] + behind:
+        used(1 - y, zz, c)
+    near.wait_recv()
+    for zz in [z] + behind:
+        used(y, zz, 1 - c)
     far.wait_recv()
-    core(place(1 - y, behind[1], c), 14)
-    use(place(1 - y, behind[1], c))
-    sources = [
-        place(y, behind[0], 1 - c),
-        place(y, behind[2], 1 - c),
-        place(1 - y, z, 1 - c),
-        place(y, behind[1], 1 - c),
-        place(1 - y, behind[0], 1 - c),
-        place(1 - y, behind[2], 1 - c),
-        place(1 - y, behind[1], 1 - c),
-    ]
-    for (copy, _), block in zip(to_core[1:], sources):
-        copy.wait_recv()
-        use(block)
-    for copy in started:
+    for zz in [z] + behind:
+        used(1 - y, zz, 1 - c)
+    for copy in sent + [near, far]:
         copy.wait_send()
 
 
@@ -197,7 +193,7 @@
     for copy in sent:
         copy.wait()
     found = jnp.dot(select, in_t[...].reshape(candidates, block), preferred_element_type=jnp.float32)
-    emb[t] = found.astype(jnp.bfloat16)
+    emb[spot(t)] = found.astype(jnp.bfloat16)
     gather_blocks(emb, t, g_send, g_recv)
 
 
@@ -243,7 +239,8 @@
     scale = lax.rsqrt(jnp.sum(squares, axis=1, keepdims=True) / (holders * block) + epsilon)
     for k in range(holders):
         at = slice(k * block, (k + 1) * block)
-        out[:, at] = (whole[k].astype(jnp.float32) * scale * gain[:, at]).astype(jnp.bfloat16)
+        scaled = whole[spot(k)].astype(jnp.float32) * scale * gain[:, at]
+        out[:, :, at] = scaled.reshape(out.shape[0], out.shape[1], block).astype(jnp.bfloat16)
 
 
 def project_kernel(mixed, weight_hbm, emb, next_gain, stream, normed, whole, weight, out_c, in_c, kept, out_z, in_z, slab, out_y, in_y, local,
@@ -291,24 +288,24 @@
     to_y.start()
     to_y.wait_recv()
     branch = slab[y] + in_y[...].astype(jnp.float32)
-    mine = (emb[t].astype(jnp.float32) + branch).astype(jnp.bfloat16)
-    stream[...] = mine
-    whole[t] = mine
+    mine = (emb[spot(t)].astype(jnp.float32) + branch).astype(jnp.bfloat16)
+    stream[...] = mine.astype(jnp.float32).reshape(stream.shape).astype(jnp.bfloat16)
+    whole[spot(t)] = mine
     gather_blocks(whole, t, g_send, g_recv)
     normalize(whole, next_gain, normed)
     for copy in to_core + to_z + [to_y]:
         copy.wait_send()
 
 
-def project(mixed, weight, emb, next_gain):
+def project(mixed, weight, emb, next_gain, steps):
     holders, rows, block = emb.shape
     bf16, f32, dma = jnp.bfloat16, jnp.float32, pltpu.SemaphoreType.DMA
     vmem, anywhere = pl.BlockSpec(memory_space=pltpu.VMEM), pl.BlockSpec(memory_space=pl.ANY)
     return pl.pallas_call(
         project_kernel,
         out_shape=(
-            jax.ShapeDtypeStruct((rows, block), bf16),
-            jax.ShapeDtypeStruct((rows, holders * block), bf16),
+            jax.ShapeDtypeStruct((rows // steps, steps, block), bf16),
+            jax.ShapeDtypeStruct((rows // steps, steps, holders * block), bf16),
         ),
         in_specs=[vmem, anywhere, vmem, vmem],
         out_specs=(vmem, vmem),
@@ -426,11 +423,11 @@
 
     squares = jnp.zeros((rows, block), jnp.float32)
     for k in range(holders):
-        wide = emb[k].astype(jnp.float32)
+        wide = emb[spot(k)].astype(jnp.float32)
         squares = squares + wide * wide
     scale = lax.rsqrt(jnp.sum(squares, axis=1, keepdims=True) / (holders * block) + epsilon)
     for k in range(holders):
-        nrm[:, k * block : (k + 1) * block] = (emb[k].astype(jnp.float32) * scale * gain[:, k * block : (k + 1) * block]).astype(jnp.bfloat16)
+        nrm[:, k * block : (k + 1) * block] = (emb[spot(k)].astype(jnp.float32) * scale * gain[:, k * block : (k + 1) * block]).astype(jnp.bfloat16)
     narrow = dtw[...].astype(jnp.float32)
     narrow = jnp.concatenate([narrow, jnp.zeros((16 - heads, narrow.shape[1]), jnp.float32)], axis=0).astype(jnp.bfloat16)
     steps_raw = lax.dot_general(nrm[...], narrow, (((1,), (1,)), ((), ())), preferred_element_type=jnp.float32)
@@ -495,12 +492,13 @@
 
 
 def fused_kernel(heads, ids_in, table_hbm, trainer_hbm, gain, weight_hbm, dtw, bias, log_rate, skip, ngain,
-                 state_hbm, oweight_hbm, next_gain, head_map, new_hbm, stream, normed, gathered, swap, need, table,
-                 trainer, weight, state, oweight, all_ids, out_d, in_d, out_t, in_t, out_r, in_r, emb, whole,
-                 swap_out, proj, narrow, raw, key, query, xin, xrow, decay, read, mixed, out_c, in_c, kept, out_z,
-                 in_z, slab, out_y, in_y, l_sem, w_sem, s_sem, n_sem, i_send, i_recv, d_send, d_recv, t_send,
-                 t_recv, r_send, r_recv, e_send, e_recv, a_send, a_recv, x_send, x_recv, c_send, c_recv, z_send,
-                 z_recv, y_send, y_recv, g_send, g_recv):
+                 state_hbm, oweight_hbm, next_gain, head_map, new_hbm, stream, normed, relaid, need, table,
+                 gathered, swap, relaid_v, trainer, weight, state, oweight, all_ids, out_d, in_d, out_t, in_t,
+                 out_r, in_r, emb, whole, swap_out, proj, narrow, raw, key, query, xin, xrow, decay, read, mixed,
+                 out_c, in_c, kept, out_z, in_z, slab, slab_b, out_y, in_y, out_yb, in_yb, out_zb, in_zb, l_sem,
+                 w_sem, s_sem, n_sem, m_sem, i_send, i_recv, d_send, d_recv, t_send, t_recv, r_send, r_recv, e_send,
+                 e_recv, a_send, a_recv, x_send, x_recv, c_send, c_recv, z_send, z_recv, y_send, y_recv, g_send,
+                 g_recv):
     bf16, f32 = jnp.bfloat16, jnp.float32
     groups, holders = in_d.shape[0], in_t.shape[0]
     vocab, width = table.shape
@@ -524,8 +522,9 @@
     ids2 = ids_in[...]
     row = jnp.concatenate([ids2[s : s + 1] for s in range(steps)], axis=1)
     all_ids[g] = jnp.broadcast_to(row, (8, rows))
-    others_d = [lax.rem(g + o, groups) for o in range(1, groups)]
-    others_t = [lax.rem(t + o, holders) for o in range(1, holders)]
+    others_d = [xx * 2 + 1 - low for xx in (lax.rem(x + 2, X), lax.rem(x + 1, X), lax.rem(x + 3, X))]
+    others_d += [x_ahead[1], x_ahead[0], x_ahead[2], beside]
+    others_t = farthest_first(t)
     greet([{"dp": d} for d in others_d] + [{"tensor": d} for d in others_t])
     moves = []
     for o, d in enumerate(others_d):
@@ -586,10 +585,10 @@
     lift = jnp.where(
         (lax.broadcasted_iota(jnp.int32, (WIDE, rows), 0) == index_row) & (once > 0.5), 1.0, 0.0
     ).astype(bf16)
-    spot = jnp.where(slot < SLOTS, from_g * (2 * SLOTS) + slot, -2 * SLOTS * groups)
-    take_low = jnp.dot(lift, jnp.where(spot == at1, 1.0, 0.0).astype(bf16), preferred_element_type=f32).astype(bf16)
+    lie = jnp.where(slot < SLOTS, from_g * (2 * SLOTS) + slot, -2 * SLOTS * groups)
+    take_low = jnp.dot(lift, jnp.where(lie == at1, 1.0, 0.0).astype(bf16), preferred_element_type=f32).astype(bf16)
     take_high = jnp.dot(
-        lift, jnp.where(spot + SLOTS == at1, 1.0, 0.0).astype(bf16), preferred_element_type=f32
+        lift, jnp.where(lie + SLOTS == at1, 1.0, 0.0).astype(bf16), preferred_element_type=f32
     ).astype(bf16)
     lower = jnp.where(
         lax.broadcasted_iota(jnp.int32, (vocab, vocab), 0) < lax.broadcasted_iota(jnp.int32, (vocab, vocab), 1),
@@ -689,14 +688,25 @@
         copy.wait()
     to_x = [share(g, 1 + o, x_ahead[o]) for o in range(X - 1)]
 
+    def relay(at):
+        piece = gathered[at].reshape(holders * trows, block)
+        relaid_v[at] = lax.dot_general(swap[...], piece, (((1,), (1,)), ((), ())), preferred_element_type=f32)
+        relaid_out(at).start()
+
+    def relaid_out(at):
+        wide = holders * trows
+        columns = pl.ds(pl.multiple_of(at * wide, wide), wide)
+        return pltpu.make_async_copy(relaid_v.at[at], relaid.at[:, columns], m_sem.at[at])
+
+
     for copy in sent:
         copy.wait()
     found = jnp.dot(select, in_t[...].reshape(holders * WIDE, block), preferred_element_type=f32)
-    emb[t] = found.astype(bf16)
-
-    def project_in(k):
-        proj[...] += jnp.dot(emb[k], weight[k], preferred_element_type=f32)
-        raw[...] += lax.dot_general(emb[k], narrow[k], (((1,), (1,)), ((), ())), preferred_element_type=f32)
+    emb[spot(t)] = found.astype(bf16)
+
+    def project_in(at, k):
+        proj[...] += jnp.dot(emb[at], weight[k], preferred_element_type=f32)
+        raw[...] += lax.dot_general(emb[at], narrow[k], (((1,), (1,)), ((), ())), preferred_element_type=f32)
 
     for copy in loads_w:
         copy.wait()
@@ -723,28 +733,35 @@
     load_oweight.wait()
     rows_in = mixed[...]
 
-    def partial_of(k, cc):
-        at = place(k % 2, k // 2, cc) * block
+    def partial_of(yy, zz, cc):
+        at = place(yy, zz, cc) * block
         return jnp.dot(rows_in, oweight[:, pl.ds(pl.multiple_of(at, block), block)], preferred_element_type=f32)
 
     to_core = []
-    for k in range(2 * Z):
-        out_c[k] = partial_of(k, 1 - c).astype(bf16)
-        to_core.append(remote(out_c.at[k], in_c.at[k], c_send.at[k], c_recv.at[k], tensor=other))
+    for n in range(2):
+        for zz in range(Z // 2):
+            for yy in range(2):
+                out_c[n, zz, yy] = partial_of(yy, n * (Z // 2) + zz, 1 - c).astype(bf16)
+        to_core.append(remote(out_c.at[n], in_c.at[n], c_send.at[n], c_recv.at[n], tensor=other))
         to_core[-1].start()
-    for k in range(2 * Z):
-        kept[k // 2, k % 2] = partial_of(k, c)
-    for k in range(2 * Z):
-        to_core[k].wait_recv()
-        total = kept[k // 2, k % 2] + in_c[k].astype(f32)
-        kept[k // 2, k % 2] = total
-        out_z[k // 2, k % 2] = total.astype(bf16)
-    to_z = []
-    for o in range(Z - 1):
-        to_z.append(
-            remote(out_z.at[ahead[o]], in_z.at[o], z_send.at[o], z_recv.at[o], tensor=place(y, ahead[o], c))
-        )
-        to_z[-1].start()
+    for zz in range(Z):
+        for yy in range(2):
+            kept[zz, yy] = partial_of(yy, zz, c)
+    cut = rows // 2
+    for n in range(2):
+        to_core[n].wait_recv()
+        for zz in range(n * (Z // 2), (n + 1) * (Z // 2)):
+            for yy in range(2):
+                total = kept[zz, yy] + in_c[n, zz % (Z // 2), yy].astype(f32)
+                kept[zz, yy] = total
+                out_z[zz, yy] = total[:cut].astype(bf16)
+                out_yb[yy, zz] = total[cut:].astype(bf16)
+    to_yb = remote(out_yb.at[1 - y], in_yb, y_send.at[0], y_recv.at[0], tensor=across)
+    to_yb.start()
+    to_z = {}
+    for o in (1, 0, 2):
+        to_z[o] = remote(out_z.at[ahead[o]], in_z.at[o], z_send.at[o], z_recv.at[o], tensor=place(y, ahead[o], c))
+        to_z[o].start()
 
     def move_on(p, carry):
         update(p, per, heads, steps, key, state, decay, xrow)
@@ -754,30 +771,52 @@
     lax.fori_loop(0, chunks // 2, move_on, 0)
     to_beside.wait_recv()
     passed = [share(beside, X + o, x_ahead[o]) for o in range(X - 1)]
-    lax.fori_loop(chunks // 2, chunks, move_on, 0)
-    for copy in residual:
-        copy.wait()
-    embedded = jnp.dot(select, in_r[...].reshape(holders * WIDE, block), preferred_element_type=f32)
-    total = kept[z]
-    for o in range(Z - 1):
+    relay(g)
+    to_yb.wait_recv()
+    for zz in range(Z):
+        total = kept[zz, y, cut:] + in_yb[zz].astype(f32)
+        slab_b[zz] = total
+        out_zb[zz] = total.astype(bf16)
+    to_zb = {}
+    for o in (1, 0, 2):
+        to_zb[o] = remote(
+            out_zb.at[ahead[o]], in_zb.at[o], z_send.at[3 + o], z_recv.at[3 + o], tensor=place(y, ahead[o], c)
+        )
+        to_zb[o].start()
+    total = kept[z, :, :cut]
+    for o in (0, 2, 1):
         to_z[o].wait_recv()
         total = total + in_z[o].astype(f32)
     slab[...] = total
     out_y[...] = slab[1 - y].astype(bf16)
-    to_y = remote(out_y, in_y, y_send.at[0], y_recv.at[0], tensor=across)
+    to_y = remote(out_y, in_y, y_send.at[1], y_recv.at[1], tensor=across)
     to_y.start()
+    lax.fori_loop(chunks // 2, chunks, move_on, 0)
+    relay(beside)
+    for o in range(X - 1):
+        to_x[o].wait_recv()
+        relay(x_behind[o])
+    for copy in residual:
+        copy.wait()
+    embedded = jnp.dot(select, in_r[...].reshape(holders * WIDE, block), preferred_element_type=f32)
+    total = slab_b[z]
+    for o in (0, 2, 1):
+        to_zb[o].wait_recv()
+        total = total + in_zb[o].astype(f32)
+    here = spot(t)
+    whole[here, cut:] = (embedded[cut:] + total).astype(bf16)
     to_y.wait_recv()
-    branch = slab[y] + in_y[...].astype(f32)
-    mine = (embedded + branch).astype(bf16)
-    stream[...] = mine
-    whole[t] = mine
-
+    whole[here, :cut] = (embedded[:cut] + (slab[y] + in_y[...].astype(f32))).astype(bf16)
+    stream[...] = whole[here].astype(f32).reshape(stream.shape).astype(bf16)
     gather_blocks(whole, t, g_send, g_recv)
+    for o in range(X - 1):
+        passed[o].wait_recv()
+        relay(x_behind[o] + 1 - 2 * low)
     normalize(whole, next_gain, normed)
-    for copy in to_x + passed:
-        copy.wait_recv()
-    for copy in to_core + to_z + [to_y] + shared:
+    for copy in to_core + list(to_z.values()) + list(to_zb.values()) + [to_yb, to_y] + shared:
         copy.wait_send()
+    for at in range(groups):
+        relaid_out(at).wait()
     for p in range(chunks):
         fresh_state(p).wait()
 
@@ -785,17 +824,22 @@
 def fused(ids, table, trainer, gain, weight, dtw, bias, log_rate, skip, ngain, state, oweight, next_gain, head_map,
           groups, holders):
     row_count, heads, state_size, head_size = state.shape
-    rows = ids.shape[0] * ids.shape[1]
+    steps = ids.shape[0]
+    rows = steps * ids.shape[1]
     vocab, width = table.shape
     block = width // holders
     trows = trainer.shape[0]
     units = heads * head_size
+    cut = rows // 2
     columns = weight.shape[1]
     bf16, f32, dma = jnp.bfloat16, jnp.float32, pltpu.SemaphoreType.DMA
     vmem, anywhere = pl.BlockSpec(memory_space=pltpu.VMEM), pl.BlockSpec(memory_space=pl.ANY)
     smem = pl.BlockSpec(memory_space=pltpu.SMEM)
     buffers = [
         ((vocab, width), bf16),
+        ((groups, holders, trows, block), bf16),
+        ((units, units), bf16),
+        ((groups, units, holders * trows), f32),
         (trainer.shape, f32),
         ((holders, block, columns), bf16),
         (state.shape, f32),
@@ -820,31 +864,36 @@
         ((heads, rows, head_size), f32),
         ((heads, rows, head_size), f32),
         ((rows, units), bf16),
-        ((2 * Z, rows, block), bf16),
-        ((2 * Z, rows, block), bf16),
+        ((2, Z // 2, 2, rows, block), bf16),
+        ((2, Z // 2, 2, rows, block), bf16),
         ((Z, 2, rows, block), f32),
-        ((Z, 2, rows, block), bf16),
-        ((Z - 1, 2, rows, block), bf16),
-        ((2, rows, block), f32),
-        ((rows, block), bf16),
-        ((rows, block), bf16),
+        ((Z, 2, cut, block), bf16),
+        ((Z - 1, 2, cut, block), bf16),
+        ((2, cut, block), f32),
+        ((Z, cut, block), f32),
+        ((cut, block), bf16),
+        ((cut, block), bf16),
+        ((2, Z, cut, block), bf16),
+        ((Z, cut, block), bf16),
+        ((Z, cut, block), bf16),
+        ((Z - 1, cut, block), bf16),
     ]
-    semaphores = [3, holders, 8, 8]
-    for count in (groups - 1, groups - 1, holders - 1, holders - 1, holders - 1, holders - 1, 2 * X - 1, 2 * Z, Z - 1, 1):
+    semaphores = [3, holders, 8, 8, groups]
+    for count in (groups - 1, groups - 1, holders - 1, holders - 1, holders - 1, holders - 1, 2 * X - 1):
         semaphores += [count, count]
-    semaphores += [holders - 1, holders - 1]
+    for count in (2, 2 * (Z - 1), 2, holders - 1):
+        semaphores += [count, count]
     return pl.pallas_call(
         functools.partial(fused_kernel, heads),
         out_shape=(
             jax.ShapeDtypeStruct(state.shape, f32),
-            jax.ShapeDtypeStruct((rows, block), bf16),
-            jax.ShapeDtypeStruct((rows, width), bf16),
-            jax.ShapeDtypeStruct((groups, holders, trows, block), bf16),
-            jax.ShapeDtypeStruct((units, units), bf16),
+            jax.ShapeDtypeStruct((row_count, steps, block), bf16),
+            jax.ShapeDtypeStruct((row_count, steps, width), bf16),
+            jax.ShapeDtypeStruct((units, width), f32),
             jax.ShapeDtypeStruct((1, 1), jnp.int32),
         ),
         in_specs=[vmem, anywhere, anywhere, vmem, anywhere, vmem, smem, smem, smem, vmem, anywhere, anywhere, vmem, vmem],
-        out_specs=(anywhere, vmem, vmem, vmem, vmem, smem),
+        out_specs=(anywhere, vmem, vmem, anywhere, smem),
         scratch_shapes=[pltpu.VMEM(*buffer) for buffer in buffers] + [dma((count,)) for count in semaphores],
         compiler_params=pltpu.CompilerParams(
             collective_id=0, has_side_effects=True, vmem_limit_bytes=60 * 2**20
@@ -877,7 +926,7 @@
     state = ssm_state.swapaxes(2, 3)
     gain, ngain, ngain_next = in_gain.reshape(1, -1), norm_gain.reshape(1, -1), next_gain.reshape(1, -1)
     mix = (in_weight, dt_weight.T, dt_bias, a_log, d_skip, ngain, state)
-    now, stream, normed, gathered, swap, need = fused(
+    now, stream, normed, relaid, need = fused(
         token_ids.T, embed_table, trainer_weight, gain, *mix, out_weight, ngain_next, head_map, groups, holders
     )
 
@@ -891,22 +940,16 @@
         empty = jnp.zeros((holders, rows, width // holders), jnp.bfloat16)
         _, emb = lax.while_loop(lambda inner: inner[0] < todo, more, (jnp.int32(0), empty))
         now, mixed = mixer(emb, gain, *mix)
-        stream, normed = project(mixed, out_weight, emb, ngain_next)
+        stream, normed = project(mixed, out_weight, emb, ngain_next, step_count)
         return jnp.int32(0), now, stream, normed
 
     _, now, stream, normed = lax.while_loop(
         lambda carry: carry[0] > 0, again, (need.reshape(()), now, stream, normed)
     )
-    relaid = lax.dot_general(
-        swap,
-        gathered.reshape(width, swap.shape[1]),
-        (((1,), (1,)), ((), ())),
-        preferred_element_type=jnp.float32,
-    )
     return (
         now.swapaxes(2, 3),
-        stream.reshape(row_count, step_count, -1),
-        normed.reshape(row_count, step_count, width),
+        stream,
+        normed,
         relaid,
     )
 

time: 87.5 us -> 82.7 us (0.945)
  matrix products: 4.5 us -> 0 us
  Pallas kernels: 75 us -> 72.3 us
  local copies, waits for them, and re-layouts: 6.08 us -> 8.6 us
    unnamed x23 -> x28, local copies, waits for them, and re-layouts: 2.06 us -> 8.6 us
    dot_general x1 -> x0, matrix products: 4.5 us -> none  [per_device(): lax.dot_general(swap, gathered.reshape(width, swap.shape[1]), (((1,), (1,...]
    reshape x2 -> x0, local copies, waits for them, and re-layouts: 4.02 us -> none  [the longest x1 2.52 us: per_device(): normed.reshape(row_count, step_count, width)]
    pallas_call x1, Pallas kernels: 75 us -> 72.3 us  [fused(): pl.pallas_call(functools.partial(fused_kernel, heads), out_shape=(jax.Sha...]
where the time goes in v4:
time: 82.7 us; the launch traced here: 82.5 us
  Pallas kernels  72.3 us (87%)
  local copies, waits for them, and re-layouts  8.6 us (10%)
    pallas_call x1, Pallas kernels, fused(): pl.pallas_call(functools.partial(fused_kernel, heads), out_shape=(jax.Sha...  72.3 us
    unnamed x28, local copies, waits for them, and re-layouts  8.6 us

profile of v4, /device:TPU:1, one launch (start us, length us, event | category | flops | bytes accessed | tf_op | source)
XLA Modules:
  0.0 82.5 jit_solution(2726981698620204041)
XLA Ops:
  0.6 0.0 copy-start
  0.6 0.0 copy-start.3
  0.7 0.0 copy-start.4
  0.7 0.0 copy-start.5
  0.7 0.0 copy-start.6
  0.7 0.0 copy-start.8
  0.7 0.0 copy-start.9
  0.7 0.0 copy-start.10
  0.7 0.0 copy-start.11
  0.7 72.3 %fused.1 = (f32[64,2,64,128]{3,2,1,0:T(8,128)}, bf16[64,2,256]{2,1,0:T(2,128)(2,1)}, bf16[64,2,4096]{2,1,0:T(2,128)(2,1)}, f32[256,4096]{1,0:T(8,128)}, s32[1,1]{1,0:T(1,128)}) custom-call(s32[2,64]{1,0:T(2,128)} %bitcast.14, bf16[512,4096]{1,0:T(8,128)(2,1)} %table_hbm.1, f32[32,4096]{1,0:T(8,128)} %trainer_hbm.1, f32[1,4096]{1,0:T(1,128)} %bitcast.16, ...), custom_call_target="tpu_custom_call" | custom-call | tf_op jit(solution)/shard_map/fused/pallas_call | solution.py:886
  73.1 0.0 copy-done
  73.1 0.0 copy-done.3
  73.1 0.0 copy-done.4
  73.1 0.0 copy-done.5
  73.1 0.0 copy-done.6
  73.1 0.0 copy-done.8
  73.1 0.0 copy-done.9
  73.1 0.0 copy-done.10
  73.1 0.0 copy-done.11
  73.2 0.8 while.22
  74.0 4.9 %copy.42 = f32[64,2,128,64]{2,3,1,0:T(8,128)} copy(f32[64,2,128,64]{2,3,1,0:T(8,128)} %bitcast.13) | data formatting | bytes 8388608
  78.9 0.6 copy.43
  79.5 1.0 %copy.44 = bf16[64,2,4096]{2,1,0:T(2,128)(2,1)} copy(bf16[64,2,4096]{2,1,0:T(2,128)(2,1)S(1)} %copy-done.2) | data formatting | bytes 2097152
  80.5 2.0 %copy.45 = f32[256,4096]{1,0:T(8,128)} copy(f32[256,4096]{1,0:T(8,128)S(1)} %copy-done.1) | data formatting | bytes 8388608
  (6 shorter events, 0.0 us)
Async XLA Ops:
  0.6 72.4 %copy-start = (bf16[256,4096]{1,0:T(8,128)(2,1)S(1)}, bf16[256,4096]{1,0:T(8,128)(2,1)}, u32[]{:S(2)}) copy-start(bf16[256,4096]{1,0:T(8,128)(2,1)} %oweight_hbm.1) | copy-start | bytes 6291460
  0.6 72.4 %copy-start.3 = (s32[64,2]{0,1:T(2,128)S(1)}, s32[64,2]{0,1:T(2,128)}, u32[]{:S(2)}) copy-start(s32[64,2]{0,1:T(2,128)} %param.18) | copy-start | bytes 1540
  0.7 72.4 %copy-start.4 = (f32[4096]{0:T(1024)S(1)}, f32[4096]{0:T(1024)}, u32[]{:S(2)}) copy-start(f32[4096]{0:T(1024)} %param.20) | copy-start | bytes 49156
  0.7 72.4 %copy-start.5 = (bf16[4096,2]{0,1:T(2,128)(2,1)S(1)}, bf16[4096,2]{0,1:T(2,128)(2,1)}, u32[]{:S(2)}) copy-start(bf16[4096,2]{0,1:T(2,128)(2,1)} %param.22) | copy-start | bytes 49156
  0.7 72.4 %copy-start.6 = (f32[4096]{0:T(1024)S(1)}, f32[4096]{0:T(1024)}, u32[]{:S(2)}) copy-start(f32[4096]{0:T(1024)} %param.28) | copy-start | bytes 49156
  0.7 72.4 %copy-start.8 = (f32[256]{0:T(256)S(1)}, f32[256]{0:T(256)}, u32[]{:S(2)}) copy-start(f32[256]{0:T(256)} %param.26) | copy-start | bytes 3076
  0.7 72.4 %copy-start.9 = (f32[2]{0:T(128)S(1)}, f32[2]{0:T(128)}, u32[]{:S(2)}) copy-start(f32[2]{0:T(128)} %bias.1) | copy-start | bytes 28
  0.7 72.4 %copy-start.10 = (f32[2]{0:T(128)S(1)}, f32[2]{0:T(128)}, u32[]{:S(2)}) copy-start(f32[2]{0:T(128)} %log_rate.1) | copy-start | bytes 28
  0.7 72.4 %copy-start.11 = (f32[2]{0:T(128)S(1)}, f32[2]{0:T(128)}, u32[]{:S(2)}) copy-start(f32[2]{0:T(128)} %skip.1) | copy-start | bytes 28
  73.9 5.0 %copy-start.7 = (bf16[64,2,256]{2,1,0:T(2,128)(2,1)S(1)}, bf16[64,2,256]{2,1,0:T(2,128)(2,1)}, u32[]{:S(2)}) copy-start(bf16[64,2,256]{2,1,0:T(2,128)(2,1)} %get-tuple-element.297) | copy-start | bytes 196612
  73.9 5.6 %copy-start.2 = (bf16[64,2,4096]{2,1,0:T(2,128)(2,1)S(1)}, bf16[64,2,4096]{2,1,0:T(2,128)(2,1)}, u32[]{:S(2)}) copy-start(bf16[64,2,4096]{2,1,0:T(2,128)(2,1)} %get-tuple-element.298) | copy-start | bytes 3145732
  73.9 6.6 %copy-start.1 = (f32[256,4096]{1,0:T(8,128)S(1)}, f32[256,4096]{1,0:T(8,128)}, u32[]{:S(2)}) copy-start(f32[256,4096]{1,0:T(8,128)} %get-tuple-element.293) | copy-start | bytes 12582916

commit v5 on v4

--- a/solution.py
+++ b/solution.py
@@ -51,7 +51,7 @@
     return [place(yy, zz, cc) for yy, zz in chips for cc in (c, 1 - c)] + [place(y, z, 1 - c)]
 
 
-def gather_blocks(buf, t, send, recv, use=lambda at, position: None):
+def gather_blocks(buf, t, send, recv, use=lambda at, position: None, meanwhile=lambda: None):
     y, z, c, ahead, behind, place = tensor_near(t)
     other = place(y, z, 1 - c)
     to = [(1 - y, ahead[1]), (1 - y, ahead[0]), (1 - y, ahead[2]), (1 - y, z), (y, ahead[1]), (y, ahead[0]), (y, ahead[2])]
@@ -71,6 +71,7 @@
         position = place(yy, zz, cc)
         use(spot(position), position)
 
+    meanwhile()
     used(y, z, c)
     for role in (5, 6, 4):
         sent[role].wait_recv()
@@ -88,8 +89,7 @@
     far.wait_recv()
     for zz in [z] + behind:
         used(1 - y, zz, 1 - c)
-    for copy in sent + [near, far]:
-        copy.wait_send()
+    return sent + [near, far]
 
 
 def order(row, column, at0, at1, vocab):
@@ -194,7 +194,8 @@
         copy.wait()
     found = jnp.dot(select, in_t[...].reshape(candidates, block), preferred_element_type=jnp.float32)
     emb[spot(t)] = found.astype(jnp.bfloat16)
-    gather_blocks(emb, t, g_send, g_recv)
+    for copy in gather_blocks(emb, t, g_send, g_recv):
+        copy.wait_send()
 
 
 def lookup(ids, table, groups, holders, start):
@@ -291,9 +292,9 @@
     mine = (emb[spot(t)].astype(jnp.float32) + branch).astype(jnp.bfloat16)
     stream[...] = mine.astype(jnp.float32).reshape(stream.shape).astype(jnp.bfloat16)
     whole[spot(t)] = mine
-    gather_blocks(whole, t, g_send, g_recv)
+    spread = gather_blocks(whole, t, g_send, g_recv)
     normalize(whole, next_gain, normed)
-    for copy in to_core + to_z + [to_y]:
+    for copy in to_core + to_z + [to_y] + spread:
         copy.wait_send()
 
 
@@ -492,13 +493,12 @@
 
 
 def fused_kernel(heads, ids_in, table_hbm, trainer_hbm, gain, weight_hbm, dtw, bias, log_rate, skip, ngain,
-                 state_hbm, oweight_hbm, next_gain, head_map, new_hbm, stream, normed, relaid, need, table,
-                 gathered, swap, relaid_v, trainer, weight, state, oweight, all_ids, out_d, in_d, out_t, in_t,
-                 out_r, in_r, emb, whole, swap_out, proj, narrow, raw, key, query, xin, xrow, decay, read, mixed,
-                 out_c, in_c, kept, out_z, in_z, slab, slab_b, out_y, in_y, out_yb, in_yb, out_zb, in_zb, l_sem,
-                 w_sem, s_sem, n_sem, m_sem, i_send, i_recv, d_send, d_recv, t_send, t_recv, r_send, r_recv, e_send,
-                 e_recv, a_send, a_recv, x_send, x_recv, c_send, c_recv, z_send, z_recv, y_send, y_recv, g_send,
-                 g_recv):
+                 state_hbm, oweight_hbm, next_gain, head_map, new_hbm, stream, normed, gathered_out, swap, need,
+                 table, gathered, trainer, weight, state, oweight, all_ids, out_d, in_d, out_t, in_t, out_r, in_r,
+                 emb, whole, swap_out, proj, narrow, raw, key, query, xin, xrow, decay, read, mixed, out_c, in_c,
+                 kept, out_z, in_z, slab, slab_b, out_y, in_y, out_yb, in_yb, out_zb, in_zb, l_sem, w_sem, s_sem,
+                 n_sem, m_sem, i_send, i_recv, d_send, d_recv, t_send, t_recv, r_send, r_recv, e_send, e_recv,
+                 a_send, a_recv, x_send, x_recv, c_send, c_recv, z_send, z_recv, y_send, y_recv, g_send, g_recv):
     bf16, f32 = jnp.bfloat16, jnp.float32
     groups, holders = in_d.shape[0], in_t.shape[0]
     vocab, width = table.shape
@@ -597,7 +597,8 @@
     ).astype(bf16)
 
     for copy in moves:
-        copy.wait()
+        copy.wait_recv()
+    owed = list(moves)
     ids_all = all_ids[0]
     at_g = lax.broadcasted_iota(jnp.int32, (8, rows), 0)
     for gg in range(1, groups):
@@ -658,7 +659,8 @@
     raw[...] = jnp.zeros_like(raw)
 
     for copy in sent:
-        copy.wait()
+        copy.wait_recv()
+    owed += sent
     arrived = in_d[...].reshape(groups * 2 * SLOTS, half)
     total = jnp.zeros((WIDE, block), f32)
     for part, take in enumerate((take_low, take_high)):
@@ -685,22 +687,20 @@
         return copy
 
     for copy in swaps:
-        copy.wait()
+        copy.wait_recv()
+    owed += swaps
     to_x = [share(g, 1 + o, x_ahead[o]) for o in range(X - 1)]
 
     def relay(at):
-        piece = gathered[at].reshape(holders * trows, block)
-        relaid_v[at] = lax.dot_general(swap[...], piece, (((1,), (1,)), ((), ())), preferred_element_type=f32)
-        relaid_out(at).start()
-
-    def relaid_out(at):
-        wide = holders * trows
-        columns = pl.ds(pl.multiple_of(at * wide, wide), wide)
-        return pltpu.make_async_copy(relaid_v.at[at], relaid.at[:, columns], m_sem.at[at])
+        pass_on(at).start()
+
+    def pass_on(at):
+        return pltpu.make_async_copy(gathered.at[at], gathered_out.at[at], m_sem.at[at])
 
 
     for copy in sent:
-        copy.wait()
+        copy.wait_recv()
+    owed += sent
     found = jnp.dot(select, in_t[...].reshape(holders * WIDE, block), preferred_element_type=f32)
     emb[spot(t)] = found.astype(bf16)
 
@@ -710,12 +710,15 @@
 
     for copy in loads_w:
         copy.wait()
-    gather_blocks(emb, t, e_send, e_recv, project_in)
     residual = []
-    for o, d in enumerate(others_t):
-        residual.append(remote(out_r.at[d], in_r.at[t], r_send.at[o], r_recv.at[o], tensor=d))
-        residual[-1].start()
-    in_r[t] = out_r[t]
+
+    def send_raw():
+        for o, d in enumerate(others_t):
+            residual.append(remote(out_r.at[d], in_r.at[t], r_send.at[o], r_recv.at[o], tensor=d))
+            residual[-1].start()
+        in_r[t] = out_r[t]
+
+    owed += gather_blocks(emb, t, e_send, e_recv, project_in, send_raw)
     to_beside = share(g, 0, beside)
     sizes = (weight.shape[2] // heads, head_size, state_size)
     for h in range(heads):
@@ -797,7 +800,8 @@
         to_x[o].wait_recv()
         relay(x_behind[o])
     for copy in residual:
-        copy.wait()
+        copy.wait_recv()
+    owed += residual
     embedded = jnp.dot(select, in_r[...].reshape(holders * WIDE, block), preferred_element_type=f32)
     total = slab_b[z]
     for o in (0, 2, 1):
@@ -808,17 +812,23 @@
     to_y.wait_recv()
     whole[here, :cut] = (embedded[:cut] + (slab[y] + in_y[...].astype(f32))).astype(bf16)
     stream[...] = whole[here].astype(f32).reshape(stream.shape).astype(bf16)
-    gather_blocks(whole, t, g_send, g_recv)
+    owed += to_core + list(to_z.values()) + list(to_zb.values()) + [to_yb, to_y]
+
+    def settle():
+        for copy in owed:
+            copy.wait_send()
+        for p in range(chunks):
+            fresh_state(p).wait()
+
+    spread = gather_blocks(whole, t, g_send, g_recv, meanwhile=settle)
     for o in range(X - 1):
         passed[o].wait_recv()
         relay(x_behind[o] + 1 - 2 * low)
     normalize(whole, next_gain, normed)
-    for copy in to_core + list(to_z.values()) + list(to_zb.values()) + [to_yb, to_y] + shared:
+    for copy in shared + spread:
         copy.wait_send()
     for at in range(groups):
-        relaid_out(at).wait()
-    for p in range(chunks):
-        fresh_state(p).wait()
+        pass_on(at).wait()
 
 
 def fused(ids, table, trainer, gain, weight, dtw, bias, log_rate, skip, ngain, state, oweight, next_gain, head_map,
@@ -838,8 +848,6 @@
     buffers = [
         ((vocab, width), bf16),
         ((groups, holders, trows, block), bf16),
-        ((units, units), bf16),
-        ((groups, units, holders * trows), f32),
         (trainer.shape, f32),
         ((holders, block, columns), bf16),
         (state.shape, f32),
@@ -889,11 +897,12 @@
             jax.ShapeDtypeStruct(state.shape, f32),
             jax.ShapeDtypeStruct((row_count, steps, block), bf16),
             jax.ShapeDtypeStruct((row_count, steps, width), bf16),
-            jax.ShapeDtypeStruct((units, width), f32),
+            jax.ShapeDtypeStruct((groups, holders, trows, block), bf16),
+            jax.ShapeDtypeStruct((units, units), bf16),
             jax.ShapeDtypeStruct((1, 1), jnp.int32),
         ),
         in_specs=[vmem, anywhere, anywhere, vmem, anywhere, vmem, smem, smem, smem, vmem, anywhere, anywhere, vmem, vmem],
-        out_specs=(anywhere, vmem, vmem, anywhere, smem),
+        out_specs=(anywhere, vmem, vmem, anywhere, vmem, smem),
         scratch_shapes=[pltpu.VMEM(*buffer) for buffer in buffers] + [dma((count,)) for count in semaphores],
         compiler_params=pltpu.CompilerParams(
             collective_id=0, has_side_effects=True, vmem_limit_bytes=60 * 2**20
@@ -926,7 +935,7 @@
     state = ssm_state.swapaxes(2, 3)
     gain, ngain, ngain_next = in_gain.reshape(1, -1), norm_gain.reshape(1, -1), next_gain.reshape(1, -1)
     mix = (in_weight, dt_weight.T, dt_bias, a_log, d_skip, ngain, state)
-    now, stream, normed, relaid, need = fused(
+    now, stream, normed, gathered, swap, need = fused(
         token_ids.T, embed_table, trainer_weight, gain, *mix, out_weight, ngain_next, head_map, groups, holders
     )
 
@@ -945,6 +954,9 @@
 
     _, now, stream, normed = lax.while_loop(
         lambda carry: carry[0] > 0, again, (need.reshape(()), now, stream, normed)
+    )
+    relaid = lax.dot_general(
+        swap, gathered.reshape(width, swap.shape[1]), (((1,), (1,)), ((), ())), preferred_element_type=jnp.float32
     )
     return (
         now.swapaxes(2, 3),

time: 82.7 us -> 78.8 us (0.953)
  local copies, waits for them, and re-layouts: 8.6 us -> 3.72 us
  matrix products: 0 us -> 4.5 us
  Pallas kernels: 72.3 us -> 68.8 us
    unnamed x28 -> x29, local copies, waits for them, and re-layouts: 8.6 us -> 3.72 us
    dot_general x0 -> x1, matrix products: none -> 4.5 us  [per_device(): lax.dot_general(swap, gathered.reshape(width, swap.shape[1]), (((1,), (1,...]
    pallas_call x1, Pallas kernels: 72.3 us -> 68.8 us  [fused(): pl.pallas_call(functools.partial(fused_kernel, heads), out_shape=(jax.Sha...]
where the time goes in v5:
time: 78.8 us; the launch traced here: 78.7 us
  Pallas kernels  68.8 us (87%)
  matrix products  4.5 us (6%)
  local copies, waits for them, and re-layouts  3.72 us (5%)
  loops' own time  0.83 us (1%)
  between operations  0.81 us (1%)
    pallas_call x1, Pallas kernels, fused(): pl.pallas_call(functools.partial(fused_kernel, heads), out_shape=(jax.Sha...  68.8 us
    dot_general x1, matrix products, per_device(): lax.dot_general(swap, gathered.reshape(width, swap.shape[1]), (((1,), (1,...  4.5 us
    unnamed x29, local copies, waits for them, and re-layouts  3.72 us

profile of v5, /device:TPU:1, one launch (start us, length us, event | category | flops | bytes accessed | tf_op | source)
XLA Modules:
  0.0 78.7 jit_solution(10089676928999280559)
XLA Ops:
  0.6 0.0 copy-start
  0.6 0.0 copy-start.3
  0.7 0.0 copy-start.4
  0.7 0.0 copy-start.5
  0.7 0.0 copy-start.6
  0.7 0.0 copy-start.9
  0.7 0.0 copy-start.10
  0.7 0.0 copy-start.11
  0.7 0.0 copy-start.12
  0.7 68.8 %fused.1 = (f32[64,2,64,128]{3,2,1,0:T(8,128)}, bf16[64,2,256]{2,1,0:T(2,128)(2,1)}, bf16[64,2,4096]{2,1,0:T(2,128)(2,1)}, bf16[8,16,32,256]{3,2,1,0:T(8,128)(2,...) custom-call(s32[2,64]{1,0:T(2,128)} %bitcast.18, bf16[512,4096]{1,0:T(8,128)(2,1)} %table_hbm.1, f32[32,4096]{1,0:T(8,128)} %trainer_hbm.1, ...), custom_call_target="tpu_custom_call" | custom-call | tf_op jit(solution)/shard_map/fused/pallas_call | solution.py:894
  69.6 0.0 copy-done
  69.6 0.0 copy-done.3
  69.6 0.0 copy-done.4
  69.6 0.0 copy-done.5
  69.6 0.0 copy-done.6
  69.6 0.0 copy-done.9
  69.6 0.0 copy-done.10
  69.7 0.8 %while.22 = (s32[]{:T(128)}, f32[64,2,64,128]{3,2,1,0:T(8,128)}, bf16[64,2,256]{2,1,0:T(2,128)(2,1)}, bf16[64,2,4096]{2,1,0:T(2,128)(2,1)}, s32[64,2]{0,1:T(2,12...) while((s32[]{:T(128)}, f32[64,2,64,128]{3,2,1,0:T(8,128)}, ...), condition=%region_3.0_spmd, body=%region_0.0_spmd | while | flops 524291 | bytes 4198700 | solution.py:955
  70.5 0.1 copy-done.7
  70.6 4.5 %fusion = f32[256,4096]{1,0:T(8,128)} fusion(bf16[256,256]{1,0:T(8,128)(2,1)S(1)} %copy-done.7, bf16[4096,256]{1,0:T(8,128)(2,1)} %bitcast.17), kind=kOutput, calls=%fused_computation | convolution fusion | flops 536870912 | bytes 6422528 | tf_op jit(solution)/shard_map/dot_general | solution.py:958
  75.1 2.0 %copy.41 = f32[64,2,128,64]{2,3,1,0:T(8,128)} copy(f32[64,2,128,64]{2,3,1,0:T(8,128)S(1)} %bitcast.16) | data formatting | bytes 8388608
  77.1 0.0 copy-done.8
  77.1 0.6 copy.42
  77.7 1.0 %copy.43 = bf16[64,2,4096]{2,1,0:T(2,128)(2,1)} copy(bf16[64,2,4096]{2,1,0:T(2,128)(2,1)S(1)} %copy-done.2) | data formatting | bytes 2097152
  (8 shorter events, 0.0 us)
Async XLA Ops:
  0.6 68.9 %copy-start = (bf16[256,4096]{1,0:T(8,128)(2,1)S(1)}, bf16[256,4096]{1,0:T(8,128)(2,1)}, u32[]{:S(2)}) copy-start(bf16[256,4096]{1,0:T(8,128)(2,1)} %oweight_hbm.1) | copy-start | bytes 6291460
  0.6 68.9 %copy-start.3 = (s32[64,2]{0,1:T(2,128)S(1)}, s32[64,2]{0,1:T(2,128)}, u32[]{:S(2)}) copy-start(s32[64,2]{0,1:T(2,128)} %param.18) | copy-start | bytes 1540
  0.7 68.9 %copy-start.4 = (f32[4096]{0:T(1024)S(1)}, f32[4096]{0:T(1024)}, u32[]{:S(2)}) copy-start(f32[4096]{0:T(1024)} %param.20) | copy-start | bytes 49156
  0.7 68.9 %copy-start.5 = (bf16[4096,2]{0,1:T(2,128)(2,1)S(1)}, bf16[4096,2]{0,1:T(2,128)(2,1)}, u32[]{:S(2)}) copy-start(bf16[4096,2]{0,1:T(2,128)(2,1)} %param.22) | copy-start | bytes 49156
  0.7 68.9 %copy-start.6 = (f32[4096]{0:T(1024)S(1)}, f32[4096]{0:T(1024)}, u32[]{:S(2)}) copy-start(f32[4096]{0:T(1024)} %param.28) | copy-start | bytes 49156
  0.7 68.9 %copy-start.9 = (f32[256]{0:T(256)S(1)}, f32[256]{0:T(256)}, u32[]{:S(2)}) copy-start(f32[256]{0:T(256)} %param.26) | copy-start | bytes 3076
  0.7 68.9 %copy-start.10 = (f32[2]{0:T(128)S(1)}, f32[2]{0:T(128)}, u32[]{:S(2)}) copy-start(f32[2]{0:T(128)} %bias.1) | copy-start | bytes 28
  0.7 68.9 %copy-start.11 = (f32[2]{0:T(128)S(1)}, f32[2]{0:T(128)}, u32[]{:S(2)}) copy-start(f32[2]{0:T(128)} %log_rate.1) | copy-start | bytes 28
  0.7 68.9 %copy-start.12 = (f32[2]{0:T(128)S(1)}, f32[2]{0:T(128)}, u32[]{:S(2)}) copy-start(f32[2]{0:T(128)} %skip.1) | copy-start | bytes 28
  69.7 0.9 %copy-start.7 = (bf16[256,256]{1,0:T(8,128)(2,1)S(1)}, bf16[256,256]{1,0:T(8,128)(2,1)}, u32[]{:S(2)}) copy-start(bf16[256,256]{1,0:T(8,128)(2,1)} %get-tuple-element.130) | copy-start | bytes 393220
  70.5 4.6 %copy-start.1 = (f32[64,2,64,128]{3,2,1,0:T(8,128)S(1)}, f32[64,2,64,128]{3,2,1,0:T(8,128)}, u32[]{:S(2)}) copy-start(f32[64,2,64,128]{3,2,1,0:T(8,128)} %get-tuple-element.298) | copy-start | bytes 12582916
  75.1 2.0 %copy-start.8 = (bf16[64,2,256]{2,1,0:T(2,128)(2,1)S(1)}, bf16[64,2,256]{2,1,0:T(2,128)(2,1)}, u32[]{:S(2)}) copy-start(bf16[64,2,256]{2,1,0:T(2,128)(2,1)} %get-tuple-element.299) | copy-start | bytes 196612
  75.1 2.7 %copy-start.2 = (bf16[64,2,4096]{2,1,0:T(2,128)(2,1)S(1)}, bf16[64,2,4096]{2,1,0:T(2,128)(2,1)}, u32[]{:S(2)}) copy-start(bf16[64,2,4096]{2,1,0:T(2,128)(2,1)} %get-tuple-element.300) | copy-start | bytes 3145732

commit v6 on v5

--- a/solution.py
+++ b/solution.py
@@ -231,12 +231,13 @@
     )(ids, start, table)
 
 
-def normalize(whole, gain, out):
+def normalize(whole, gain, out, squares=None):
     holders, rows, block = whole.shape
-    squares = jnp.zeros((rows, block), jnp.float32)
-    for k in range(holders):
-        wide = whole[k].astype(jnp.float32)
-        squares = squares + wide * wide
+    if squares is None:
+        squares = jnp.zeros((rows, block), jnp.float32)
+        for k in range(holders):
+            wide = whole[k].astype(jnp.float32)
+            squares = squares + wide * wide
     scale = lax.rsqrt(jnp.sum(squares, axis=1, keepdims=True) / (holders * block) + epsilon)
     for k in range(holders):
         at = slice(k * block, (k + 1) * block)
@@ -573,23 +574,6 @@
         before = jnp.where((row_t == column_t) & (row < column), fits, 0.0)
         return once, slot, jnp.sum(before, axis=1, keepdims=True).astype(jnp.int32)
 
-    column = jnp.broadcast_to(row, (8, rows)).astype(f32).T.astype(jnp.int32)[:, 0:1]
-    once, slot, index = places(row, column)
-    from_t, from_g = lax.rem(column // vocab, holders), column // (vocab * holders)
-    comes = (slot < SLOTS) & (index < WIDE)
-    want = jnp.where(comes, from_t * WIDE + index, -1)
-    select = jnp.where(want == lax.broadcasted_iota(jnp.int32, (rows, holders * WIDE), 1), 1.0, 0.0).astype(bf16)
-    permute = jnp.where(at1 == lax.rem(at0, steps) * row_count + at0 // steps, 1.0, 0.0).astype(bf16)
-    select = jnp.dot(permute, select, preferred_element_type=f32).astype(bf16)
-    index_row = turn(jnp.where((from_t == t) & comes, index, -1))
-    lift = jnp.where(
-        (lax.broadcasted_iota(jnp.int32, (WIDE, rows), 0) == index_row) & (once > 0.5), 1.0, 0.0
-    ).astype(bf16)
-    lie = jnp.where(slot < SLOTS, from_g * (2 * SLOTS) + slot, -2 * SLOTS * groups)
-    take_low = jnp.dot(lift, jnp.where(lie == at1, 1.0, 0.0).astype(bf16), preferred_element_type=f32).astype(bf16)
-    take_high = jnp.dot(
-        lift, jnp.where(lie + SLOTS == at1, 1.0, 0.0).astype(bf16), preferred_element_type=f32
-    ).astype(bf16)
     lower = jnp.where(
         lax.broadcasted_iota(jnp.int32, (vocab, vocab), 0) < lax.broadcasted_iota(jnp.int32, (vocab, vocab), 1),
         1.0,
@@ -635,6 +619,23 @@
         sent[-1].start()
     in_d[g] = out_d[g]
 
+    column = jnp.broadcast_to(row, (8, rows)).astype(f32).T.astype(jnp.int32)[:, 0:1]
+    once, slot, index = places(row, column)
+    from_t, from_g = lax.rem(column // vocab, holders), column // (vocab * holders)
+    comes = (slot < SLOTS) & (index < WIDE)
+    want = jnp.where(comes, from_t * WIDE + index, -1)
+    select = jnp.where(want == lax.broadcasted_iota(jnp.int32, (rows, holders * WIDE), 1), 1.0, 0.0).astype(bf16)
+    permute = jnp.where(at1 == lax.rem(at0, steps) * row_count + at0 // steps, 1.0, 0.0).astype(bf16)
+    select = jnp.dot(permute, select, preferred_element_type=f32).astype(bf16)
+    index_row = turn(jnp.where((from_t == t) & comes, index, -1))
+    lift = jnp.where(
+        (lax.broadcasted_iota(jnp.int32, (WIDE, rows), 0) == index_row) & (once > 0.5), 1.0, 0.0
+    ).astype(bf16)
+    lie = jnp.where(slot < SLOTS, from_g * (2 * SLOTS) + slot, -2 * SLOTS * groups)
+    take_low = jnp.dot(lift, jnp.where(lie == at1, 1.0, 0.0).astype(bf16), preferred_element_type=f32).astype(bf16)
+    take_high = jnp.dot(
+        lift, jnp.where(lie + SLOTS == at1, 1.0, 0.0).astype(bf16), preferred_element_type=f32
+    ).astype(bf16)
     most = jnp.zeros((1, 1), jnp.int32)
     over = jnp.zeros((1, 1), jnp.int32)
     for gg in range(groups):
@@ -698,6 +699,8 @@
         return pltpu.make_async_copy(gathered.at[at], gathered_out.at[at], m_sem.at[at])
 
 
+    for copy in loads_w:
+        copy.wait()
     for copy in sent:
         copy.wait_recv()
     owed += sent
@@ -708,8 +711,6 @@
         proj[...] += jnp.dot(emb[at], weight[k], preferred_element_type=f32)
         raw[...] += lax.dot_general(emb[at], narrow[k], (((1,), (1,)), ((), ())), preferred_element_type=f32)
 
-    for copy in loads_w:
-        copy.wait()
     residual = []
 
     def send_raw():
@@ -820,11 +821,17 @@
         for p in range(chunks):
             fresh_state(p).wait()
 
-    spread = gather_blocks(whole, t, g_send, g_recv, meanwhile=settle)
+    squares = [jnp.zeros((rows, block), f32)]
+
+    def square(at, position):
+        wide = whole[at].astype(f32)
+        squares[0] = squares[0] + wide * wide
+
+    spread = gather_blocks(whole, t, g_send, g_recv, square, settle)
     for o in range(X - 1):
         passed[o].wait_recv()
         relay(x_behind[o] + 1 - 2 * low)
-    normalize(whole, next_gain, normed)
+    normalize(whole, next_gain, normed, squares[0])
     for copy in shared + spread:
         copy.wait_send()
     for at in range(groups):

time: 78.8 us -> 79.1 us (level)
  no operation moved by 1% of the time
where the time goes in v6:
time: 79.1 us; the launch traced here: 78.9 us
  Pallas kernels  69.1 us (87%)
  matrix products  4.5 us (6%)
  local copies, waits for them, and re-layouts  3.72 us (5%)
  loops' own time  0.83 us (1%)
  between operations  0.81 us (1%)
    pallas_call x1, Pallas kernels, fused(): pl.pallas_call(functools.partial(fused_kernel, heads), out_shape=(jax.Sha...  69.1 us
    dot_general x1, matrix products, per_device(): lax.dot_general(swap, gathered.reshape(width, swap.shape[1]), (((1,), (1,...  4.5 us
    unnamed x29, local copies, waits for them, and re-layouts  3.72 us

profile of v6, /device:TPU:1, one launch (start us, length us, event | category | flops | bytes accessed | tf_op | source)
XLA Modules:
  0.0 78.9 jit_solution(14438078224115690830)
XLA Ops:
  0.6 0.0 copy-start
  0.6 0.0 copy-start.3
  0.7 0.0 copy-start.4
  0.7 0.0 copy-start.5
  0.7 0.0 copy-start.6
  0.7 0.0 copy-start.9
  0.7 0.0 copy-start.10
  0.7 0.0 copy-start.11
  0.7 0.0 copy-start.12
  0.7 69.1 %fused.1 = (f32[64,2,64,128]{3,2,1,0:T(8,128)}, bf16[64,2,256]{2,1,0:T(2,128)(2,1)}, bf16[64,2,4096]{2,1,0:T(2,128)(2,1)}, bf16[8,16,32,256]{3,2,1,0:T(8,128)(2,...) custom-call(s32[2,64]{1,0:T(2,128)} %bitcast.18, bf16[512,4096]{1,0:T(8,128)(2,1)} %table_hbm.1, f32[32,4096]{1,0:T(8,128)} %trainer_hbm.1, ...), custom_call_target="tpu_custom_call" | custom-call | tf_op jit(solution)/shard_map/fused/pallas_call | solution.py:901
  69.8 0.0 copy-done
  69.8 0.0 copy-done.3
  69.8 0.0 copy-done.4
  69.8 0.0 copy-done.5
  69.8 0.0 copy-done.6
  69.8 0.0 copy-done.9
  69.9 0.8 %while.22 = (s32[]{:T(128)}, f32[64,2,64,128]{3,2,1,0:T(8,128)}, bf16[64,2,256]{2,1,0:T(2,128)(2,1)}, bf16[64,2,4096]{2,1,0:T(2,128)(2,1)}, s32[64,2]{0,1:T(2,12...) while((s32[]{:T(128)}, f32[64,2,64,128]{3,2,1,0:T(8,128)}, ...), condition=%region_3.0_spmd, body=%region_0.0_spmd | while | flops 524291 | bytes 4198700 | solution.py:962
  70.7 0.0 copy-start.1
  70.7 0.1 copy-done.7
  70.8 4.5 %fusion = f32[256,4096]{1,0:T(8,128)} fusion(bf16[256,256]{1,0:T(8,128)(2,1)S(1)} %copy-done.7, bf16[4096,256]{1,0:T(8,128)(2,1)} %bitcast.17), kind=kOutput, calls=%fused_computation | convolution fusion | flops 536870912 | bytes 6422528 | tf_op jit(solution)/shard_map/dot_general | solution.py:965
  75.3 2.0 %copy.41 = f32[64,2,128,64]{2,3,1,0:T(8,128)} copy(f32[64,2,128,64]{2,3,1,0:T(8,128)S(1)} %bitcast.16) | data formatting | bytes 8388608
  77.3 0.0 copy-done.8
  77.3 0.6 copy.42
  77.9 1.0 %copy.43 = bf16[64,2,4096]{2,1,0:T(2,128)(2,1)} copy(bf16[64,2,4096]{2,1,0:T(2,128)(2,1)S(1)} %copy-done.2) | data formatting | bytes 2097152
  (8 shorter events, 0.0 us)
Async XLA Ops:
  0.6 69.2 %copy-start = (bf16[256,4096]{1,0:T(8,128)(2,1)S(1)}, bf16[256,4096]{1,0:T(8,128)(2,1)}, u32[]{:S(2)}) copy-start(bf16[256,4096]{1,0:T(8,128)(2,1)} %oweight_hbm.1) | copy-start | bytes 6291460
  0.6 69.2 %copy-start.3 = (s32[64,2]{0,1:T(2,128)S(1)}, s32[64,2]{0,1:T(2,128)}, u32[]{:S(2)}) copy-start(s32[64,2]{0,1:T(2,128)} %param.18) | copy-start | bytes 1540
  0.7 69.2 %copy-start.4 = (f32[4096]{0:T(1024)S(1)}, f32[4096]{0:T(1024)}, u32[]{:S(2)}) copy-start(f32[4096]{0:T(1024)} %param.20) | copy-start | bytes 49156
  0.7 69.2 %copy-start.5 = (bf16[4096,2]{0,1:T(2,128)(2,1)S(1)}, bf16[4096,2]{0,1:T(2,128)(2,1)}, u32[]{:S(2)}) copy-start(bf16[4096,2]{0,1:T(2,128)(2,1)} %param.22) | copy-start | bytes 49156
  0.7 69.2 %copy-start.6 = (f32[4096]{0:T(1024)S(1)}, f32[4096]{0:T(1024)}, u32[]{:S(2)}) copy-start(f32[4096]{0:T(1024)} %param.28) | copy-start | bytes 49156
  0.7 69.2 %copy-start.9 = (f32[256]{0:T(256)S(1)}, f32[256]{0:T(256)}, u32[]{:S(2)}) copy-start(f32[256]{0:T(256)} %param.26) | copy-start | bytes 3076
  0.7 69.2 %copy-start.10 = (f32[2]{0:T(128)S(1)}, f32[2]{0:T(128)}, u32[]{:S(2)}) copy-start(f32[2]{0:T(128)} %bias.1) | copy-start | bytes 28
  0.7 69.2 %copy-start.11 = (f32[2]{0:T(128)S(1)}, f32[2]{0:T(128)}, u32[]{:S(2)}) copy-start(f32[2]{0:T(128)} %log_rate.1) | copy-start | bytes 28
  0.7 69.2 %copy-start.12 = (f32[2]{0:T(128)S(1)}, f32[2]{0:T(128)}, u32[]{:S(2)}) copy-start(f32[2]{0:T(128)} %skip.1) | copy-start | bytes 28
  69.9 0.9 %copy-start.7 = (bf16[256,256]{1,0:T(8,128)(2,1)S(1)}, bf16[256,256]{1,0:T(8,128)(2,1)}, u32[]{:S(2)}) copy-start(bf16[256,256]{1,0:T(8,128)(2,1)} %get-tuple-element.130) | copy-start | bytes 393220
  70.7 4.6 %copy-start.1 = (f32[64,2,64,128]{3,2,1,0:T(8,128)S(1)}, f32[64,2,64,128]{3,2,1,0:T(8,128)}, u32[]{:S(2)}) copy-start(f32[64,2,64,128]{3,2,1,0:T(8,128)} %get-tuple-element.298) | copy-start | bytes 12582916
  75.3 2.0 %copy-start.8 = (bf16[64,2,256]{2,1,0:T(2,128)(2,1)S(1)}, bf16[64,2,256]{2,1,0:T(2,128)(2,1)}, u32[]{:S(2)}) copy-start(bf16[64,2,256]{2,1,0:T(2,128)(2,1)} %get-tuple-element.299) | copy-start | bytes 196612
  75.3 2.7 %copy-start.2 = (bf16[64,2,4096]{2,1,0:T(2,128)(2,1)S(1)}, bf16[64,2,4096]{2,1,0:T(2,128)(2,1)}, u32[]{:S(2)}) copy-start(bf16[64,2,4096]{2,1,0:T(2,128)(2,1)} %get-tuple-element.300) | copy-start | bytes 3145732
